TPU v7x, 512 devices: a whole 4x4x16 slice. The times are simulated.
512 devices in a mesh: pair: 32 (over y, z_hi, core), tm: 16 (over z_lo, x).
Axes of the slice: x: 4, y: 4, z: 16 (z_hi: 4, z_lo: 4; z = z_hi * 4 + z_lo), core: 2. Of those that a mesh axis runs over, the one named last changes fastest.
Arguments:
- samples: float32 [2048, 16384], P('pair', 'tm'), may hold values from -1100 to 1100
- tile_rows: int32 [128], replicated, may hold values from 0 to 63, as said below
- tile_offsets: int32 [128], replicated, may hold values from -31 to 31
- tile_live: int32 [128], replicated, may hold values from 0 to 1, as said below
Outputs:
- correlations: float32 [128, 256, 1024], P('pair', 'tm')
Inputs may be any that keep to these rules, and one draw needn't show every extreme that they name: `tile_rows`: blocks a and a + offset of a tile lie in 0 to 63 and fewer than 32 apart. Block q belongs to index q // 2 of pair. The live tiles of one index of pair name different blocks, at most 1 of them held by any one index of pair, and in every draw some index names exactly 1 held by one index. `tile_live`: slots are live from the first slot of an index of pair onward; every index has at least 2 live slots and some index has all 4 live.
All inputs are finite; a program needn't handle non-finite values.
Results may differ from a plain program's by a relative error of at most 0.02.
Values may be sent and summed in bfloat16 or wider, within the bound.
No kernel may reach another device: no remote copies, remote signals or barrier semaphores. Data moves between devices by JAX's collectives and lax.ppermute only.
A program may use at most 64 MiB of HBM per device.

v0:
```python
import math

import jax
import jax.numpy as jnp
from jax import lax
from jax.sharding import PartitionSpec as P

CB = 32
LAG = 128


def with_halo(cells, sides, width):
    for axis, dim in sides:
        count = lax.axis_size(axis)
        ends = count - 1
        head = lax.slice_in_dim(cells, 0, width, axis=dim)
        tail = lax.slice_in_dim(cells, cells.shape[dim] - width, cells.shape[dim], axis=dim)
        cells = jnp.concatenate(
            [
                lax.ppermute(tail, axis, [(i, (i + 1) % count) for i in range(ends)]),
                cells,
                lax.ppermute(head, axis, [((i + 1) % count, i) for i in range(ends)]),
            ],
            axis=dim,
        )
    return cells


def lag_products(middle, window_rows):
    length = middle.shape[1]
    lag_count = window_rows.shape[1] - length
    result = lax.conv_general_dilated(
        window_rows[:, None, :],
        middle[:, None, :],
        (1,),
        "VALID",
        dimension_numbers=("NCW", "OIW", "WCN"),
        preferred_element_type=jnp.float32,
    )
    return result[:lag_count].reshape(lag_count, middle.shape[0] * window_rows.shape[0])


def body(samples, tile_rows, tile_offsets, tile_live):
    local_rows, length = samples.shape
    tm_count = lax.axis_size("tm")
    pair_count = lax.axis_size("pair")
    my_pair = lax.axis_index("pair")
    whole_length = length * tm_count
    moments = lax.psum((jnp.sum(samples, axis=1), jnp.sum(samples * samples, axis=1)), "tm")
    average = moments[0] / whole_length
    power_mean = moments[1] / whole_length
    scaling = lax.rsqrt(power_mean - average * average + 1e-05)
    whitened = ((samples - average[:, None]) * scaling[:, None]).astype(jnp.bfloat16)
    framed = with_halo(whitened, (("tm", 1),), LAG)
    frame_width = framed.shape[1]
    slot_count = tile_rows.shape[0] // pair_count
    first_rows = tile_rows.reshape(pair_count, slot_count)
    second_rows = first_rows + tile_offsets.reshape(pair_count, slot_count)
    wanted = jnp.stack([first_rows, second_rows], axis=2).reshape(pair_count, 2 * slot_count)
    live_slots = tile_live.reshape(pair_count, slot_count)
    live_sides = jnp.repeat(live_slots, 2, axis=1)
    my_wanted = lax.dynamic_index_in_dim(wanted, my_pair, 0, keepdims=False)
    my_sides = lax.dynamic_index_in_dim(live_sides, my_pair, 0, keepdims=False) > 0
    my_slots = lax.dynamic_index_in_dim(live_slots, my_pair, 0, keepdims=False)
    everything = lax.all_gather(framed, "pair", axis=0, tiled=True)
    block_count = everything.shape[0] // CB
    block_table = everything.reshape(block_count, CB * frame_width)
    picker = (my_wanted[:, None] == jnp.arange(block_count, dtype=jnp.int32)[None, :]) & my_sides[
        :, None
    ]
    picked = jnp.dot(
        picker.astype(jnp.bfloat16), block_table, preferred_element_type=jnp.float32
    ).astype(jnp.bfloat16)
    picked = picked.reshape(slot_count, 2, CB, frame_width)
    lag_count = frame_width - length
    factor = 1.0 / math.sqrt(whole_length)

    def live_work(operands):
        return lag_products(operands[0][:, LAG : LAG + length], operands[1]) * factor

    def dead_work(operands):
        return jnp.zeros((lag_count, CB * CB), jnp.float32)

    partial_list = []
    for slot_index in range(slot_count):
        partial_list.append(
            lax.cond(
                my_slots[slot_index] > 0,
                live_work,
                dead_work,
                (picked[slot_index, 0], picked[slot_index, 1]),
            )
        )
    partials = jnp.stack(partial_list)
    summed = lax.psum(partials.astype(jnp.bfloat16), "tm").astype(jnp.float32)
    lag_share = lag_count // tm_count
    return lax.dynamic_slice_in_dim(summed, lax.axis_index("tm") * lag_share, lag_share, 1)


def solution(mesh):
    in_specs = (P("pair", "tm"), P(), P(), P())
    out_specs = P("pair", "tm", None)
    return jax.shard_map(body, mesh=mesh, in_specs=in_specs, out_specs=out_specs, check_vma=False)
```

profile of v0, /device:TPU:8, one launch (start us, length us, event | category | flops | bytes accessed | tf_op | source)
XLA Modules:
  0.0 673.5 jit_solution(5322638089156802615)
XLA Ops:
  6.5 1.1 fusion.5
  7.6 44.6 %all-reduce = (f32[64]{0:T(128)S(1)}, f32[64]{0:T(128)S(1)}) all-reduce(f32[64]{0:T(128)S(1)} %get-tuple-element.42, f32[64]{0:T(128)S(1)} %get-tuple-element.41), channel_id=1, replica_groups=mesh['pair'=32,'tm'=16] {'tm'}, use_global_device_ids=true, to_apply=%region_3.0 | all-reduce | flops 128 | bytes 1024 | tf_op jit(solution)/shard_map/psum | solution.py:49
  53.3 1.3 collective-permute-start
  54.6 1.3 collective-permute-start.1
  56.0 4.2 collective-permute-done.1
  67.1 101.2 %all-gather.2.cloned.1.call-done = bf16[2048,1280]{1,0:T(8,128)(2,1)} async-done(((bf16[64,1280]{1,0:T(8,128)(2,1)}), bf16[2048,1280]{1,0:T(8,128)(2,1)}) %all-gather.2.cloned.1.call-update) | async-done | bytes 5242896 | tf_op jit(solution)/shard_map/all_gather | solution.py:65
  168.3 8.1 %reshape.119 = bf16[64,40960]{1,0:T(8,128)(2,1)} reshape(bf16[2048,1280]{1,0:T(8,128)(2,1)} %all-gather.2.cloned.1.call-done) | data formatting | bytes 10485760 | tf_op jit(solution)/shard_map/reshape | solution.py:67
  176.4 3.3 convolution_convert_fusion
  179.8 79.6 %conditional.4 = (bf16[1,256,1024]{1,2,0:T(8,128)(2,1)}) conditional(s32[]{:T(128)} %bitcast.16, () %tuple.33, bf16[4,2,32,1280]{3,2,1,0:T(8,128)(2,1)S(1)} %bitcast.46), branch_computations={%region_4.5_spmd, %region_5.6_spmd} | conditional | flops 537395200 | bytes 2473992 | solution.py:87
  180.4 1.1 copy.66
  181.4 55.8 %convolution_multiply_fusion = bf16[256,32,32]{1,2,0:T(8,128)(2,1)S(1)} fusion(bf16[32,1,1280]{0,1,2:T(2,128)(2,1)S(1)} %copy.65, bf16[32,1,1024]{0,1,2:T(2,128)(2,1)} %copy.66), kind=kOutput, calls=%fused_computation | convolution fusion | flops 537395200 | bytes 671744 | tf_op jit(solution)/shard_map/cond/branch_1_fun/slice | solution.py:40
  237.2 2.9 copy.67
  259.4 2.0 copy.79
  261.4 79.4 %conditional.5 = (bf16[1,256,1024]{1,2,0:T(8,128)(2,1)}) conditional(s32[]{:T(128)} %bitcast.19, () %tuple.34, bf16[4,2,32,1280]{3,2,1,0:T(8,128)(2,1)S(1)} %bitcast.47), branch_computations={%region_6.7_spmd, %region_7.8_spmd} | conditional | flops 537395200 | bytes 2473992 | solution.py:87
  262.0 1.1 copy.69
  263.0 55.6 %convolution_multiply_fusion.1 = bf16[256,32,32]{1,2,0:T(8,128)(2,1)S(1)} fusion(bf16[32,1,1280]{0,1,2:T(2,128)(2,1)S(1)} %copy.68, bf16[32,1,1024]{0,1,2:T(2,128)(2,1)} %copy.69), kind=kOutput, calls=%fused_computation.4 | convolution fusion | flops 537395200 | bytes 671744 | tf_op jit(solution)/shard_map/cond/branch_1_fun/slice | solution.py:40
  318.7 2.9 copy.70
  340.8 2.1 copy.80
  342.9 80.1 %conditional.6 = (bf16[1,256,1024]{1,2,0:T(8,128)(2,1)}) conditional(s32[]{:T(128)} %bitcast.20, () %tuple.35, bf16[4,2,32,1280]{3,2,1,0:T(8,128)(2,1)S(1)} %bitcast.48), branch_computations={%region_8.9_spmd, %region_9.10_spmd} | conditional | flops 537395200 | bytes 2473992 | solution.py:87
  343.4 1.1 copy.72
  344.5 55.6 %convolution_multiply_fusion.2 = bf16[256,32,32]{1,2,0:T(8,128)(2,1)S(1)} fusion(bf16[32,1,1280]{0,1,2:T(2,128)(2,1)S(1)} %copy.71, bf16[32,1,1024]{0,1,2:T(2,128)(2,1)} %copy.72), kind=kOutput, calls=%fused_computation.8 | convolution fusion | flops 537395200 | bytes 671744 | tf_op jit(solution)/shard_map/cond/branch_1_fun/slice | solution.py:40
  400.1 2.9 copy.73
  423.0 2.0 copy.81
  425.1 62.1 %conditional.7 = (bf16[1,256,1024]{1,2,0:T(8,128)(2,1)}) conditional(s32[]{:T(128)} %bitcast.21, () %tuple.36, bf16[4,2,32,1280]{3,2,1,0:T(8,128)(2,1)S(1)} %bitcast.49), branch_computations={%region_10.11_spmd, %region_11.12_spmd} | conditional | flops 537395200 | bytes 2473992 | solution.py:87
  425.1 1.2 copy.74
  426.3 1.1 copy.75
  427.4 56.9 %convolution_multiply_fusion.3 = bf16[256,32,32]{1,2,0:T(8,128)(2,1)S(1)} fusion(bf16[32,1,1280]{0,1,2:T(2,128)(2,1)} %copy.74, bf16[32,1,1024]{0,1,2:T(2,128)(2,1)} %copy.75), kind=kOutput, calls=%fused_computation.12 | convolution fusion | flops 537395200 | bytes 671744 | tf_op jit(solution)/shard_map/cond/branch_1_fun/slice | solution.py:40
  484.2 2.9 copy.76
  487.2 1.2 copy.82
  488.4 2.6 pad_maximum_fusion
  491.1 173.8 %all-reduce.3.cloned.1.call-done = bf16[4,256,1024]{2,1,0:T(8,128)(2,1)} async-done(((bf16[4,256,1024]{2,1,0:T(8,128)(2,1)}), bf16[4,256,1024]{2,1,0:T(8,128)(2,1)}) %all-reduce.3.cloned.1.call-update) | async-done | bytes 2097168 | tf_op jit(solution)/shard_map/psum | solution.py:95
  664.9 1.6 dynamic-slice_convert_fusion
  (37 shorter events, 7.1 us)
Async XLA Ops:
  6.5 161.8 %all-gather.2.cloned.1.call-start = ((), (), s32[]{:S(2)}) async-start(), calls=%async_computation | async-start | bytes 5406720 | tf_op jit(solution)/shard_map/all_gather | solution.py:65
  53.3 2.7 collective-permute-start
  54.6 5.6 collective-permute-start.1
  61.0 603.9 %all-reduce.3.cloned.1.call-start = ((), (), s32[]{:S(2)}) async-start(), calls=%async_computation.1 | async-start | bytes 4194304 | tf_op jit(solution)/shard_map/psum | solution.py:95
  425.1 63.4 %copy-start = (bf16[1,256,1024]{2,1,0:T(8,128)(2,1)S(1)}, bf16[1,256,1024]{2,1,0:T(8,128)(2,1)}, u32[]{:S(2)}) copy-start(bf16[1,256,1024]{2,1,0:T(8,128)(2,1)} %copy.79) | copy-start | bytes 1572868
  425.1 63.4 %copy-start.1 = (bf16[1,256,1024]{2,1,0:T(8,128)(2,1)S(1)}, bf16[1,256,1024]{2,1,0:T(8,128)(2,1)}, u32[]{:S(2)}) copy-start(bf16[1,256,1024]{2,1,0:T(8,128)(2,1)} %copy.80) | copy-start | bytes 1572868
Sparse Core Ops, SparseCore 0:
  61.1 107.1 all-gather.1
  491.2 173.5 all-reduce.2
where the time goes:
time: 677 us; the launch traced here: 674 us
  waiting for transfers between devices  279 us (41%)
  matrix products  227 us (34%)
  loops' own time  58.5 us (9%)
  blocking collectives  44.6 us (7%)
  local copies, waits for them, and re-layouts  37.7 us (6%)
  between operations  16.3 us (2%)
  other arithmetic  7.28 us (1%)
    slice x4, matrix products, lag_products(): result[:lag_count]  224 us
    psum x1, waiting for transfers between devices, body(): summed = lax.psum(partials.astype(jnp.bfloat16), 'tm').astype(jnp.float32)  174 us
    all_gather x1, waiting for transfers between devices, body(): everything = lax.all_gather(framed, 'pair', axis=0, tiled=True)  101 us
    another operation x4, loops' own time, body(): lax.cond(my_slots[slot_index] > 0, live_work, dead_work, (picked[slot_ind...  58.5 us
    psum x1, blocking collectives, body(): lax.psum((jnp.sum(samples, axis=1), jnp.sum(samples * samples, axis=1)),...  44.6 us
  transfers between devices with their start and end apart: 4, of which 4 were waited for; matrix products, arithmetic and copies ran while one was open for 1% of the time, Pallas kernels for 0%

commit v1 on v0

v1 whole, which is shorter than its diff:
```python
import math

import jax
import jax.numpy as jnp
from jax import lax
from jax.experimental import pallas as pl
from jax.experimental.pallas import tpu as pltpu
from jax.sharding import Mesh
from jax.sharding import PartitionSpec as P

CB = 32
LAG = 128
LANES = 128
Y, ZH, CORE, ZL, X = 4, 4, 2, 4, 4
AXES = ("y", "zh", "core", "zl", "x")
PAIRS = Y * ZH * CORE
TMS = ZL * X
EIGHTHS = Y * CORE
CHUNKS = X * EIGHTHS
FINE = 8
MEDIUM = LANES // FINE
MIB = 1 << 20

VMEM = pl.BlockSpec(memory_space=pltpu.VMEM)
SMEM = pl.BlockSpec(memory_space=pltpu.SMEM)


def whiten_kernel(count, x_ref, sums_ref, out_ref):
    rows = x_ref.shape[0]
    total = jnp.sum(sums_ref[...], axis=0, keepdims=True) / count
    square = pltpu.roll(jnp.broadcast_to(total, (8, LANES)), rows, axis=1)
    first = jnp.broadcast_to(total, (8, LANES))
    scaling = lax.rsqrt(square - first * first + 1e-05)
    row = lax.broadcasted_iota(jnp.int32, (8, LANES), 0)
    both = jnp.where(row == 0, first, scaling)
    turned = jnp.transpose(jnp.concatenate([both] * (LANES // 8), axis=0))
    average = turned[:rows, 0:1]
    scale = turned[:rows, 1:2]
    for part in range(EIGHTHS):
        piece = x_ref[:, part * LANES : (part + 1) * LANES]
        white = ((piece - average) * scale).astype(jnp.bfloat16)
        for zh in range(ZH):
            out_ref[part // CORE, zh, part % CORE] = white


def select_kernel(rows_ref, offsets_ref, table_ref, out_ref):
    zh = lax.axis_index("zh")
    blocks = table_ref.shape[0]

    def one(index, carry):
        place = index // X
        slot = index % X
        pair = (place // CORE * ZH + zh) * CORE + place % CORE
        tile = pair * X + slot
        first = rows_ref[tile]
        second = first + offsets_ref[tile]
        out_ref[2 * index] = table_ref[jnp.clip(first, 0, blocks - 1)]
        out_ref[2 * index + 1] = table_ref[jnp.clip(second, 0, blocks - 1)]
        return carry

    lax.fori_loop(0, EIGHTHS * X, one, 0)


def chunk_place(chunk):
    return chunk % EIGHTHS * X + chunk // EIGHTHS


def lag_kernel(factor, live_ref, data_ref, before_ref, after_ref, out_ref, wide_a, wide_b):
    pair = (lax.axis_index("y") * ZH + lax.axis_index("zh")) * CORE + lax.axis_index("core")
    alive = live_ref[pair * X + lax.axis_index("x")]
    width = (CHUNKS + 1) * LANES

    @pl.when(alive <= 0)
    def _():
        out_ref[...] = jnp.zeros_like(out_ref)

    @pl.when(alive > 0)
    def _():
        lane = lax.broadcasted_iota(jnp.int32, (CB, LANES), 1)
        zero = jnp.zeros((CB, LANES), jnp.float32)

        def first_chunk(chunk):
            return data_ref[chunk_place(chunk), :CB].astype(jnp.float32)

        def second_chunk(chunk):
            if chunk < 0:
                return before_ref[...].astype(jnp.float32)
            if chunk >= CHUNKS:
                return after_ref[...].astype(jnp.float32)
            return data_ref[chunk_place(chunk), CB:].astype(jnp.float32)

        for chunk in range(CHUNKS + 1):
            here = first_chunk(chunk) if chunk < CHUNKS else zero
            past = first_chunk(chunk - 1) if chunk > 0 else zero
            for step in range(MEDIUM):
                shift = step * FINE
                mixed = jnp.where(lane < LANES - shift, here, past)
                turned = pltpu.roll(mixed, shift, axis=1) if shift else here
                wide_a[step * CB : (step + 1) * CB, chunk * LANES : (chunk + 1) * LANES] = (
                    turned.astype(jnp.bfloat16)
                )
        for chunk in range(-1, CHUNKS + 1):
            here = second_chunk(chunk)
            later = second_chunk(chunk + 1) if chunk < CHUNKS else zero
            for step in range(FINE):
                mixed = jnp.where(lane >= step, here, later)
                turned = pltpu.roll(mixed, LANES - step, axis=1) if step else here
                wide_b[
                    step * CB : (step + 1) * CB, (chunk + 1) * LANES : (chunk + 2) * LANES
                ] = turned.astype(jnp.bfloat16)
        for half in range(2):
            result = lax.dot_general(
                wide_a[...],
                wide_b[:, half * LANES : half * LANES + width],
                (((1,), (1,)), ((), ())),
                preferred_element_type=jnp.float32,
            )
            rounded = (result * factor).astype(jnp.bfloat16)
            for part in range(TMS // 2):
                out_ref[half * (TMS // 2) + part] = rounded[part * 2 * CB : (part + 1) * 2 * CB]


def finish_kernel(got_ref, out_ref, grid_ref, turn_ref):
    lane = lax.broadcasted_iota(jnp.int32, (8, LANES), 1)
    for slot in range(X):
        total = got_ref[slot].astype(jnp.float32)
        for zl in range(1, ZL):
            total = total + got_ref[zl * X + slot].astype(jnp.float32)
        for g in range(2):
            grid_ref[g * 2 * CB : (g + 1) * 2 * CB] = total[:, g * LANES : (g + 1) * LANES]
        for half in range(2):
            parts = [
                [
                    grid_ref[pl.ds((2 * g + half) * CB + r, 8, stride=4), :]
                    for g in range(2)
                ]
                for r in range(4)
            ]
            for q in range(FINE):
                line = None
                for r in range(4):
                    piece = parts[r][q // 4]
                    shift = (CB * (r - q % 4)) % LANES
                    piece = pltpu.roll(piece, shift, axis=1) if shift else piece
                    line = piece if line is None else jnp.where(lane >= r * CB, piece, line)
                turn_ref[q * 8 : (q + 1) * 8, :] = line
            for k in range(8):
                out_ref[slot, half * 8 : half * 8 + 8, k * LANES : (k + 1) * LANES] = turn_ref[
                    pl.ds(k, 8, stride=8), :
                ]


def body(samples, tile_rows, tile_offsets, tile_live):
    local_rows, length = samples.shape
    whole_length = length * TMS
    bf16 = jnp.bfloat16
    sums = jnp.concatenate([jnp.sum(samples, axis=1), jnp.sum(samples * samples, axis=1)])
    with jax.named_scope("moments"):
        sums = lax.all_to_all(
            jnp.broadcast_to(sums[None], (TMS, 2 * local_rows)), ("zl", "x"), 0, 0, tiled=True
        )
    white = pl.pallas_call(
        lambda *refs: whiten_kernel(float(whole_length), *refs),
        out_shape=jax.ShapeDtypeStruct((Y, ZH, CORE, local_rows, LANES), bf16),
        in_specs=[VMEM, VMEM],
        out_specs=VMEM,
        name="whiten",
    )(samples, sums)
    with jax.named_scope("spread"):
        table = lax.all_to_all(
            white.reshape(PAIRS, local_rows, LANES), ("y", "zh", "core"), 0, 0, tiled=True
        )
    chosen = pl.pallas_call(
        select_kernel,
        out_shape=jax.ShapeDtypeStruct((CHUNKS * 2, CB, LANES), bf16),
        in_specs=[SMEM, SMEM, VMEM],
        out_specs=VMEM,
        name="select",
    )(tile_rows, tile_offsets, table.reshape(PAIRS * local_rows // CB, CB, LANES))
    with jax.named_scope("collect"):
        data = lax.all_to_all(
            chosen.reshape(CHUNKS, 2 * CB, LANES), ("y", "core", "x"), 0, 0, tiled=True
        )
    with jax.named_scope("halo"):
        before = lax.ppermute(
            data[chunk_place(CHUNKS - 1), CB:], "zl", [(i, i + 1) for i in range(ZL - 1)]
        )
        after = lax.ppermute(data[chunk_place(0), CB:], "zl", [(i + 1, i) for i in range(ZL - 1)])
    partial = pl.pallas_call(
        lambda *refs: lag_kernel(1.0 / math.sqrt(whole_length), *refs),
        out_shape=jax.ShapeDtypeStruct((TMS, 2 * CB, FINE * CB), bf16),
        in_specs=[SMEM, VMEM, VMEM, VMEM],
        out_specs=VMEM,
        scratch_shapes=[
            pltpu.VMEM((MEDIUM * CB, (CHUNKS + 1) * LANES), bf16),
            pltpu.VMEM((FINE * CB, (CHUNKS + 2) * LANES), bf16),
        ],
        compiler_params=pltpu.CompilerParams(vmem_limit_bytes=40 * MIB),
        name="lags",
    )(tile_live, data, before, after)
    with jax.named_scope("reduce"):
        got = lax.all_to_all(partial, ("zl", "x"), 0, 0, tiled=True)
    return pl.pallas_call(
        finish_kernel,
        out_shape=jax.ShapeDtypeStruct((X, 2 * FINE, CB * CB), jnp.float32),
        in_specs=[VMEM],
        out_specs=VMEM,
        scratch_shapes=[
            pltpu.VMEM((4 * CB, LANES), jnp.float32),
            pltpu.VMEM((FINE * 8, LANES), jnp.float32),
        ],
        name="finish",
    )(got)


def solution(mesh):
    devices = mesh.devices.reshape(Y, ZH, CORE, ZL, X)
    spread = Mesh(devices, AXES)
    pair, tm = ("y", "zh", "core"), ("zl", "x")
    return jax.shard_map(
        body,
        mesh=spread,
        in_specs=(P(pair, tm), P(), P(), P()),
        out_specs=P(pair, tm, None),
        check_vma=False,
    )
```

time: 677 us -> 120 us (0.18)
  the two profiles are of different devices: /device:TPU:8 before, /device:TPU:32 now
where the time goes in v1:
time: 120 us; the launch traced here: 119 us
  blocking collectives  100 us (83%)
  Pallas kernels  10.2 us (8%)
  starting transfers between devices  5.96 us (5%)
  waiting for transfers between devices  1.61 us (1%)
    all_to_all x1, blocking collectives, body(): lax.all_to_all(white.reshape(PAIRS, local_rows, LANES), ('y', 'zh', 'core...  49.4 us
    all_to_all x1, blocking collectives, body(): got = lax.all_to_all(partial, ('zl', 'x'), 0, 0, tiled=True)  19 us
    all_to_all x1, blocking collectives, body(): lax.all_to_all(chosen.reshape(CHUNKS, 2 * CB, LANES), ('y', 'core', 'x'),...  16.5 us
    all_to_all x1, blocking collectives, body(): lax.all_to_all(jnp.broadcast_to(sums[None], (TMS, 2 * local_rows)), ('zl'...  15.1 us
    ppermute x1, starting transfers between devices, body(): lax.ppermute(data[chunk_place(CHUNKS - 1), CB:], 'zl', [(i, i + 1) for i...  3.92 us
    pallas_call x1, Pallas kernels, body(): pl.pallas_call(lambda *refs: lag_kernel(1.0 / math.sqrt(whole_length), *r...  3.49 us
    pallas_call x1, Pallas kernels, body(): pl.pallas_call(select_kernel, out_shape=jax.ShapeDtypeStruct((CHUNKS * 2,...  2.67 us
  transfers between devices with their start and end apart: 2, of which 1 were waited for; matrix products, arithmetic and copies ran while one was open for 0% of the time, Pallas kernels for 0%

profile of v1, /device:TPU:32, one launch (start us, length us, event | category | flops | bytes accessed | tf_op | source)
XLA Modules:
  0.0 119.1 jit_solution(3884871746610280930)
XLA Ops:
  0.0 1.1 fusion
  1.1 0.1 pad_maximum_fusion
  1.2 15.1 %all_to_all.23 = f32[16,1,128]{2,1,0:T(1,128)} all-to-all(f32[16,1,128]{2,1,0:T(1,128)S(1)} %broadcast_in_dim.2), channel_id=1, replica_groups=mesh['y'=4,'zh'=4,'core'=2,'zl'=4,'x'=4] {'zl','x'}, dimensions={0} | all-to-all | bytes 16384 | tf_op jit(solution)/shard_map/moments/all_to_all | solution.py:159
  16.3 2.0 %whiten.1 = bf16[4,4,2,64,128]{4,3,2,1,0:T(8,128)(2,1)} custom-call(f32[64,1024]{1,0:T(8,128)} %refs_0_.2, f32[16,128]{1,0:T(8,128)} %bitcast.11), custom_call_target="tpu_custom_call" | custom-call | tf_op jit(solution)/shard_map/whiten/pallas_call | solution.py:162
  18.3 49.4 %all_to_all.24 = bf16[32,64,128]{2,1,0:T(8,128)(2,1)} all-to-all(bf16[32,64,128]{2,1,0:T(8,128)(2,1)} %bitcast.10), channel_id=1, replica_groups=mesh['y'=4,'zh'=4,'core'=2,'zl'=4,'x'=4] {'y','zh','core'}, dimensions={0} | all-to-all | bytes 1048576 | tf_op jit(solution)/shard_map/spread/all_to_all | solution.py:170
  67.7 2.7 %select.1 = bf16[64,32,128]{2,1,0:T(8,128)(2,1)} custom-call(s32[128]{0:T(128)} %rows_ref.1, s32[128]{0:T(128)} %offsets_ref.1, bf16[64,32,128]{2,1,0:T(8,128)(2,1)} %bitcast.8), custom_call_target="tpu_custom_call" | custom-call | tf_op jit(solution)/shard_map/select/pallas_call | solution.py:173
  70.4 16.5 %all_to_all.25.refs_1_ = bf16[32,64,128]{2,1,0:T(8,128)(2,1)S(1)} all-to-all(bf16[32,64,128]{2,1,0:T(8,128)(2,1)} %bitcast.9), channel_id=1, replica_groups=mesh['y'=4,'zh'=4,'core'=2,'zl'=4,'x'=4] {'y','core','x'}, dimensions={0} | all-to-all | bytes 1048576 | tf_op jit(solution)/shard_map/collect/all_to_all | solution.py:181
  86.9 0.0 copy-start
  86.9 2.0 %collective-permute-start.1 = (bf16[32,128]{1,0:T(8,128)(2,1)S(1)}, bf16[32,128]{1,0:T(8,128)(2,1)S(1)}, u32[]{:S(2)}, u32[]{:S(2)}) collective-permute-start(bf16[32,128]{1,0:T(8,128)(2,1)S(1)} %get-tuple-element.7), channel_id=1, source_target_pairs={{4,0},{8,4},{12,8},{5,1},{9,5},{13,9},{6,2},{10,6},{14,10},{7,3},{... | collective-permute-start | bytes 24584 | tf_op jit(solution)/shard_map/halo/ppermute | solution.py:188
  89.0 3.9 %collective-permute-start = (bf16[32,128]{1,0:T(8,128)(2,1)S(1)}, bf16[32,128]{1,0:T(8,128)(2,1)S(1)}, u32[]{:S(2)}, u32[]{:S(2)}) collective-permute-start(bf16[32,128]{1,0:T(8,128)(2,1)S(1)} %get-tuple-element.8), channel_id=1, source_target_pairs={{0,4},{4,8},{8,12},{1,5},{5,9},{9,13},{2,6},{6,10},{10,14},{3,7},{... | collective-permute-start | bytes 24584 | tf_op jit(solution)/shard_map/halo/ppermute | solution.py:185
  92.9 0.0 collective-permute-done.1.refs_3_
  92.9 1.6 %collective-permute-done.refs_2_ = bf16[32,128]{1,0:T(8,128)(2,1)S(1)} collective-permute-done((bf16[32,128]{1,0:T(8,128)(2,1)S(1)}, bf16[32,128]{1,0:T(8,128)(2,1)S(1)}, u32[]{:S(2)}, u32[]{:S(2)}) %collective-permute-start) | collective-permute-done | bytes 8224 | tf_op jit(solution)/shard_map/halo/ppermute | solution.py:185
  94.5 0.0 copy-done
  94.5 3.5 %lags.1 = bf16[16,64,256]{2,1,0:T(8,128)(2,1)S(1)} custom-call(s32[128]{0:T(128)S(1)} %copy-done, bf16[32,64,128]{2,1,0:T(8,128)(2,1)S(1)} %all_to_all.25.refs_1_, bf16[32,128]{1,0:T(8,128)(2,1)S(1)} %collective-permute-done.refs_2_, bf16[32,128]{1,0:T(8,128)(2,1)S(1)} %collective-permute-done.1.refs_3_), custom_call_target="tpu_custom_call" | custom-call | tf_op jit(solution)/shard_map/lags/pallas_call | solution.py:189
  98.0 19.0 %all_to_all.26.got_ref = bf16[16,64,256]{2,1,0:T(8,128)(2,1)} all-to-all(bf16[16,64,256]{2,1,0:T(8,128)(2,1)S(1)} %lags.1), channel_id=1, replica_groups=mesh['y'=4,'zh'=4,'core'=2,'zl'=4,'x'=4] {'zl','x'}, dimensions={0} | all-to-all | bytes 1048576 | tf_op jit(solution)/shard_map/reduce/all_to_all | solution.py:202
  117.0 2.1 %finish.1 = f32[4,16,1024]{2,1,0:T(8,128)} custom-call(bf16[16,64,256]{2,1,0:T(8,128)(2,1)} %all_to_all.26.got_ref), custom_call_target="tpu_custom_call" | custom-call | tf_op jit(solution)/shard_map/finish/pallas_call | solution.py:203
  (2 shorter events, 0.0 us)
Async XLA Ops:
  86.9 7.6 %copy-start = (s32[128]{0:T(128)S(1)}, s32[128]{0:T(128)}, u32[]{:S(2)}) copy-start(s32[128]{0:T(128)} %refs_0_.3) | copy-start | bytes 1540
  86.9 6.0 %collective-permute-start.1 = (bf16[32,128]{1,0:T(8,128)(2,1)S(1)}, bf16[32,128]{1,0:T(8,128)(2,1)S(1)}, u32[]{:S(2)}, u32[]{:S(2)}) collective-permute-start(bf16[32,128]{1,0:T(8,128)(2,1)S(1)} %get-tuple-element.7), channel_id=1, source_target_pairs={{4,0},{8,4},{12,8},{5,1},{9,5},{13,9},{6,2},{10,6},{14,10},{7,3},{... | collective-permute-start | bytes 24584 | tf_op jit(solution)/shard_map/halo/ppermute | solution.py:188
  89.0 5.5 %collective-permute-start = (bf16[32,128]{1,0:T(8,128)(2,1)S(1)}, bf16[32,128]{1,0:T(8,128)(2,1)S(1)}, u32[]{:S(2)}, u32[]{:S(2)}) collective-permute-start(bf16[32,128]{1,0:T(8,128)(2,1)S(1)} %get-tuple-element.8), channel_id=1, source_target_pairs={{0,4},{4,8},{8,12},{1,5},{5,9},{9,13},{2,6},{6,10},{10,14},{3,7},{... | collective-permute-start | bytes 24584 | tf_op jit(solution)/shard_map/halo/ppermute | solution.py:185

commit v2 on v1

v2 whole, which is shorter than its diff:
```python
import math

import jax
import jax.numpy as jnp
from jax import lax
from jax.experimental import pallas as pl
from jax.experimental.pallas import tpu as pltpu
from jax.sharding import Mesh
from jax.sharding import PartitionSpec as P

CB = 32
LAG = 128
LANES = 128
Y, ZH, CORE, ZL, X = 4, 4, 2, 4, 4
AXES = ("y", "zh", "core", "zl", "x")
PAIRS = Y * ZH * CORE
TMS = ZL * X
EIGHTHS = Y * CORE
CHUNKS = X * EIGHTHS
FINE = 8
MEDIUM = LANES // FINE
EXTRA = 8
ROWS = 2 * CB + EXTRA
MIB = 1 << 20

VMEM = pl.BlockSpec(memory_space=pltpu.VMEM)
SMEM = pl.BlockSpec(memory_space=pltpu.SMEM)


def split_kernel(x_ref, out_ref, extra_ref):
    rows, length = x_ref.shape
    mean = jnp.sum(x_ref[...], axis=1, keepdims=True) / length
    spread = jnp.zeros((rows, 1), jnp.float32)
    for part in range(EIGHTHS):
        piece = x_ref[:, part * LANES : (part + 1) * LANES] - mean
        spread = spread + jnp.sum(piece * piece, axis=1, keepdims=True)
        out_ref[part] = piece.astype(jnp.bfloat16)
    lane = lax.broadcasted_iota(jnp.int32, (rows, LANES), 1)
    columns = jnp.where(lane == 0, mean, jnp.where(lane == 1, spread, 0.0))
    turned = jnp.transpose(jnp.concatenate([columns] * (LANES // rows), axis=0))
    wide = lax.broadcasted_iota(jnp.int32, (1, LANES), 1)
    line = jnp.where(wide < rows, turned[0:1], turned[1:2])
    high = line.astype(jnp.bfloat16).astype(jnp.float32)
    middle = (line - high).astype(jnp.bfloat16).astype(jnp.float32)
    low = line - high - middle
    row = lax.broadcasted_iota(jnp.int32, (EXTRA, LANES), 0) % (EXTRA // 2)
    lines = jnp.where(row == 0, high, jnp.where(row == 1, middle, jnp.where(row == 2, low, 0.0)))
    extra_ref[...] = lines.astype(jnp.bfloat16)


def select_kernel(rows_ref, offsets_ref, table_ref, out_ref):
    zh = lax.axis_index("zh")
    here = lax.axis_index("y") * CORE + lax.axis_index("core")
    bulk = EIGHTHS * 2 * CB
    row = lax.broadcasted_iota(jnp.int32, (EXTRA, LANES), 0)

    def fetch(block):
        block = jnp.clip(block, 0, 2 * PAIRS - 1)
        place = ((block >> 4) << 1) | ((block >> 1) & 1)
        column = (block >> 2) & (ZH - 1)
        start = pl.multiple_of(((place << 1) | (block & 1)) * CB, CB)
        data = table_ref[column, pl.ds(start, CB)]
        lines = table_ref[column, bulk:]
        lines = jnp.where(place == here, lines, jnp.zeros_like(lines))
        return data, lines

    def one(index, carry):
        place = index >> 2
        pair = (((place >> 1) * ZH + zh) << 1) | (place & 1)
        tile = pair * X + (index & (X - 1))
        first = rows_ref[tile]
        data, lines = fetch(first)
        data_second, lines_second = fetch(first + offsets_ref[tile])
        out_ref[index, :CB] = data
        out_ref[index, CB : 2 * CB] = data_second
        out_ref[index, 2 * CB :] = jnp.where(row < EXTRA // 2, lines, lines_second)
        return carry

    lax.fori_loop(0, EIGHTHS * X, one, 0, unroll=4)


def chunk_place(chunk):
    return chunk % EIGHTHS * X + chunk // EIGHTHS


def scales(edge_ref, side, half, zl, length):
    lines = []
    for part in range(TMS):
        start = 2 * CB + part % X * EXTRA
        lines.append(edge_ref[part // X, start : start + EXTRA].astype(jnp.float32))
    base = side * (EXTRA // 2)
    sums = [line[base : base + 1] + (line[base + 1 : base + 2] + line[base + 2 : base + 3]) for line in lines]
    sums = jnp.concatenate(sums, axis=0)
    sums = jnp.where(half > 0, pltpu.roll(sums, LANES - CB, axis=1), sums)
    squares = jnp.sum(pltpu.roll(sums, LANES // 2, axis=1), axis=0, keepdims=True)
    apart = sums - jnp.sum(sums, axis=0, keepdims=True) / TMS
    power = (squares / length + jnp.sum(apart * apart, axis=0, keepdims=True)) / TMS
    scaling = lax.rsqrt(power + 1e-05)
    place = lax.broadcasted_iota(jnp.int32, (TMS, LANES), 0)
    row = lax.broadcasted_iota(jnp.int32, (8, LANES), 0)
    packed = jnp.broadcast_to(scaling, (8, LANES))
    for column in range(X + 2):
        wanted = zl * X + column - 1
        one = jnp.sum(jnp.where(place == wanted, apart, 0.0), axis=0, keepdims=True)
        packed = jnp.where(row == column + 1, one, packed)
    lane = lax.broadcasted_iota(jnp.int32, (8, LANES), 1)
    packed = jnp.where(lane < CB, packed, 0.0)
    return jnp.transpose(jnp.concatenate([packed] * (LANES // 8), axis=0))[:CB, :8]


def lag_kernel(length, rows_ref, offsets_ref, live_ref, data_ref, edge_ref, out_ref, wide_a, wide_b):
    zl = lax.axis_index("zl")
    pair = (lax.axis_index("y") * ZH + lax.axis_index("zh")) * CORE + lax.axis_index("core")
    tile = pair * X + lax.axis_index("x")
    alive = live_ref[tile]
    first_half = lax.rem(rows_ref[tile], 2)
    second_half = lax.rem(rows_ref[tile] + offsets_ref[tile] + PAIRS * 2, 2)
    width = (CHUNKS + 1) * LANES
    factor = 1.0 / math.sqrt(length * TMS)

    @pl.when(alive <= 0)
    def _():
        out_ref[...] = jnp.zeros_like(out_ref)

    @pl.when(alive > 0)
    def _():
        lane = lax.broadcasted_iota(jnp.int32, (CB, LANES), 1)
        zero = jnp.zeros((CB, LANES), jnp.float32)
        first_scale = scales(edge_ref, 0, first_half, zl, length)
        second_scale = scales(edge_ref, 1, second_half, zl, length)

        def white(piece, scale, column):
            shifted = piece.astype(jnp.float32) + scale[:, column + 2 : column + 3]
            return shifted * scale[:, 0:1]

        def first_chunk(chunk):
            return white(data_ref[chunk_place(chunk), :CB], first_scale, chunk // EIGHTHS)

        def second_chunk(chunk):
            if chunk < 0:
                piece = white(edge_ref[jnp.maximum(zl - 1, 0), CB : 2 * CB], second_scale, -1)
                return jnp.where(zl > 0, piece, 0.0)
            if chunk >= CHUNKS:
                piece = white(edge_ref[jnp.minimum(zl + 1, ZL - 1), :CB], second_scale, X)
                return jnp.where(zl < ZL - 1, piece, 0.0)
            return white(data_ref[chunk_place(chunk), CB : 2 * CB], second_scale, chunk // EIGHTHS)

        here = zero
        for chunk in range(CHUNKS + 1):
            past = here
            here = first_chunk(chunk) if chunk < CHUNKS else zero
            for step in range(MEDIUM):
                shift = step * FINE
                mixed = jnp.where(lane < LANES - shift, here, past)
                turned = pltpu.roll(mixed, shift, axis=1) if shift else here
                wide_a[step * CB : (step + 1) * CB, chunk * LANES : (chunk + 1) * LANES] = (
                    turned.astype(jnp.bfloat16)
                )
        later = second_chunk(-1)
        for chunk in range(-1, CHUNKS + 1):
            here = later
            later = second_chunk(chunk + 1) if chunk < CHUNKS else zero
            for step in range(FINE):
                mixed = jnp.where(lane >= step, here, later)
                turned = pltpu.roll(mixed, LANES - step, axis=1) if step else here
                wide_b[
                    step * CB : (step + 1) * CB, (chunk + 1) * LANES : (chunk + 2) * LANES
                ] = turned.astype(jnp.bfloat16)
        for half in range(2):
            result = lax.dot_general(
                wide_a[...],
                wide_b[:, half * LANES : half * LANES + width],
                (((1,), (1,)), ((), ())),
                preferred_element_type=jnp.float32,
            )
            rounded = (result * factor).astype(jnp.bfloat16)
            for part in range(TMS // 2):
                out_ref[half * (TMS // 2) + part] = rounded[part * 2 * CB : (part + 1) * 2 * CB]


def finish_kernel(got_ref, out_ref, grid_ref, turn_ref):
    lane = lax.broadcasted_iota(jnp.int32, (8, LANES), 1)
    for slot in range(X):
        total = got_ref[slot].astype(jnp.float32)
        for zl in range(1, ZL):
            total = total + got_ref[zl * X + slot].astype(jnp.float32)
        for g in range(2):
            grid_ref[g * 2 * CB : (g + 1) * 2 * CB] = total[:, g * LANES : (g + 1) * LANES]
        for half in range(2):
            parts = [
                [
                    grid_ref[pl.ds((2 * g + half) * CB + r, 8, stride=4), :]
                    for g in range(2)
                ]
                for r in range(4)
            ]
            for q in range(FINE):
                line = None
                for r in range(4):
                    piece = parts[r][q // 4]
                    shift = (CB * (r - q % 4)) % LANES
                    piece = pltpu.roll(piece, shift, axis=1) if shift else piece
                    line = piece if line is None else jnp.where(lane >= r * CB, piece, line)
                turn_ref[q * 8 : (q + 1) * 8, :] = line
            for k in range(8):
                out_ref[slot, half * 8 : half * 8 + 8, k * LANES : (k + 1) * LANES] = turn_ref[
                    pl.ds(k, 8, stride=8), :
                ]


def body(samples, tile_rows, tile_offsets, tile_live):
    length = samples.shape[1]
    bf16 = jnp.bfloat16
    parts, lines = pl.pallas_call(
        split_kernel,
        out_shape=(
            jax.ShapeDtypeStruct((EIGHTHS, 2 * CB, LANES), bf16),
            jax.ShapeDtypeStruct((EXTRA, LANES), bf16),
        ),
        in_specs=[VMEM],
        out_specs=(VMEM, VMEM),
        name="split",
    )(samples)
    with jax.named_scope("spread_y"):
        table = lax.all_to_all(parts, ("y", "core"), 0, 0, tiled=True)
    with jax.named_scope("spread_z"):
        table = jnp.concatenate([table.reshape(EIGHTHS * 2 * CB, LANES), lines])
        table = lax.all_gather(table, "zh")
    chosen = pl.pallas_call(
        select_kernel,
        out_shape=jax.ShapeDtypeStruct((CHUNKS, ROWS, LANES), bf16),
        in_specs=[SMEM, SMEM, VMEM],
        out_specs=VMEM,
        name="select",
    )(tile_rows, tile_offsets, table)
    with jax.named_scope("collect"):
        data = lax.all_to_all(chosen, ("y", "core", "x"), 0, 0, tiled=True)
    with jax.named_scope("edges"):
        sums = jnp.sum(data[:, 2 * CB :].reshape(EIGHTHS, X * EXTRA, LANES), axis=0)
        edges = jnp.concatenate(
            [data[chunk_place(0), CB : 2 * CB], data[chunk_place(CHUNKS - 1), CB : 2 * CB], sums]
        )
        edges = lax.all_to_all(
            jnp.broadcast_to(edges[None], (ZL,) + edges.shape), "zl", 0, 0, tiled=True
        )
    partial = pl.pallas_call(
        lambda *refs: lag_kernel(length, *refs),
        out_shape=jax.ShapeDtypeStruct((TMS, 2 * CB, FINE * CB), bf16),
        in_specs=[SMEM, SMEM, SMEM, VMEM, VMEM],
        out_specs=VMEM,
        scratch_shapes=[
            pltpu.VMEM((MEDIUM * CB, (CHUNKS + 1) * LANES), bf16),
            pltpu.VMEM((FINE * CB, (CHUNKS + 2) * LANES), bf16),
        ],
        compiler_params=pltpu.CompilerParams(vmem_limit_bytes=40 * MIB),
        name="lags",
    )(tile_rows, tile_offsets, tile_live, data, edges)
    with jax.named_scope("reduce"):
        got = lax.all_to_all(partial, ("zl", "x"), 0, 0, tiled=True)
    return pl.pallas_call(
        finish_kernel,
        out_shape=jax.ShapeDtypeStruct((X, 2 * FINE, CB * CB), jnp.float32),
        in_specs=[VMEM],
        out_specs=VMEM,
        scratch_shapes=[
            pltpu.VMEM((4 * CB, LANES), jnp.float32),
            pltpu.VMEM((FINE * 8, LANES), jnp.float32),
        ],
        name="finish",
    )(got)


def solution(mesh):
    devices = mesh.devices.reshape(Y, ZH, CORE, ZL, X)
    spread = Mesh(devices, AXES)
    pair, tm = ("y", "zh", "core"), ("zl", "x")
    return jax.shard_map(
        body,
        mesh=spread,
        in_specs=(P(pair, tm), P(), P(), P()),
        out_specs=P(pair, tm, None),
        check_vma=False,
    )
```

time: 120 us -> 102 us (0.85)
  blocking collectives: 100 us -> 90.5 us
  starting transfers between devices: 5.96 us -> 0 us
  waiting for transfers between devices: 1.61 us -> 0 us
    all_to_all x3, blocking collectives: 81 us -> 39.4 us  [the longest x1 17.7 us: body(): data = lax.all_to_all(chosen, ('y', 'core', 'x'), 0, 0, tiled=True)]
    all_gather x0 -> x1, blocking collectives: none -> 32.9 us  [body(): table = lax.all_gather(table, 'zh')]
    ppermute x2 -> x0, starting transfers between devices: 5.96 us -> none  [the longest x1 3.92 us: body(): lax.ppermute(data[chunk_place(CHUNKS - 1), CB:], 'zl', [(i, i + 1) for i...]
    ppermute x2 -> x0, waiting for transfers between devices: 1.61 us -> none  [the longest x1 1.6 us: body(): lax.ppermute(data[chunk_place(CHUNKS - 1), CB:], 'zl', [(i, i + 1) for i...]
  transfers between devices with their start and end apart: 2 -> 0, of which waited for: 1 -> 0; matrix products, arithmetic and copies ran while one was open for 0% -> 0% of each run, Pallas kernels for 0% -> 0%
where the time goes in v2:
time: 102 us
  blocking collectives  90.5 us (89%)
  Pallas kernels  10.3 us (10%)
    all_gather x1, blocking collectives, body(): table = lax.all_gather(table, 'zh')  32.9 us
    all_to_all x1, blocking collectives, body(): got = lax.all_to_all(partial, ('zl', 'x'), 0, 0, tiled=True)  18.2 us
    all_to_all x1, blocking collectives, body(): data = lax.all_to_all(chosen, ('y', 'core', 'x'), 0, 0, tiled=True)  17.7 us
    all_to_all x1, blocking collectives, body(): lax.all_to_all(jnp.broadcast_to(edges[None], (ZL,) + edges.shape), 'zl',...  11.1 us
    all_to_all x1, blocking collectives, body(): table = lax.all_to_all(parts, ('y', 'core'), 0, 0, tiled=True)  10.6 us
    pallas_call x1, Pallas kernels, body(): pl.pallas_call(lambda *refs: lag_kernel(length, *refs), out_shape=jax.Sha...  3.99 us
    pallas_call x1, Pallas kernels, body(): pl.pallas_call(select_kernel, out_shape=jax.ShapeDtypeStruct((CHUNKS, ROW...  2.48 us
    pallas_call x1, Pallas kernels, body(): pl.pallas_call(finish_kernel, out_shape=jax.ShapeDtypeStruct((X, 2 * FINE...  2.05 us

profile of v2, /device:TPU:32, one launch (start us, length us, event | category | flops | bytes accessed | tf_op | source)
XLA Modules:
  0.0 101.7 jit_solution(7775157204984744657)
XLA Ops:
  0.0 1.8 %split.1 = (bf16[8,64,128]{2,1,0:T(8,128)(2,1)}, bf16[8,128]{1,0:T(8,128)(2,1)}) custom-call(f32[64,1024]{1,0:T(8,128)} %x_ref.1), custom_call_target="tpu_custom_call" | custom-call | tf_op jit(solution)/shard_map/split/pallas_call | solution.py:214
  1.8 10.6 %all_to_all.20 = bf16[8,64,128]{2,1,0:T(8,128)(2,1)S(1)} all-to-all(bf16[8,64,128]{2,1,0:T(8,128)(2,1)} %get-tuple-element.7), channel_id=1, replica_groups=mesh['y'=4,'zh'=4,'core'=2,'zl'=4,'x'=4] {'y','core'}, dimensions={0} | all-to-all | bytes 262144 | tf_op jit(solution)/shard_map/spread_y/all_to_all | solution.py:225
  12.4 0.0 copy-start.3
  12.4 0.7 copy-done.3
  13.1 32.9 %all-gather = bf16[2080,128]{1,0:T(8,128)(2,1)} all-gather(bf16[520,128]{1,0:T(8,128)(2,1)S(1)} %pad_maximum_fusion), channel_id=2, replica_groups=mesh['y'=4,'zh'=4,'core'=2,'zl'=4,'x'=4] {'zh'}, dimensions={0}, use_global_device_ids=true | all-gather | bytes 665600 | tf_op jit(solution)/shard_map/spread_z/all_gather | solution.py:228
  46.0 2.5 %select.1 = bf16[32,72,128]{2,1,0:T(8,128)(2,1)} custom-call(s32[128]{0:T(128)} %refs_0_.1, s32[128]{0:T(128)} %refs_1_.1, bf16[4,520,128]{2,1,0:T(8,128)(2,1)} %bitcast.9), custom_call_target="tpu_custom_call" | custom-call | tf_op jit(solution)/shard_map/select/pallas_call | solution.py:229
  48.5 17.7 %all_to_all.21.refs_3_ = bf16[32,72,128]{2,1,0:T(8,128)(2,1)S(1)} all-to-all(bf16[32,72,128]{2,1,0:T(8,128)(2,1)} %select.1), channel_id=1, replica_groups=mesh['y'=4,'zh'=4,'core'=2,'zl'=4,'x'=4] {'y','core','x'}, dimensions={0} | all-to-all | bytes 1179648 | tf_op jit(solution)/shard_map/collect/all_to_all | solution.py:237
  66.3 0.0 copy-start
  66.3 0.0 copy-start.1
  66.3 0.0 copy-start.2
  66.3 11.1 %all_to_all.22.refs_4_ = bf16[4,96,128]{2,1,0:T(8,128)(2,1)S(1)} all-to-all(bf16[4,96,128]{2,1,0:T(8,128)(2,1)S(1)} %broadcast_in_dim.2), channel_id=1, replica_groups=mesh['y'=4,'zh'=4,'core'=2,'zl'=4,'x'=4] {'zl'}, dimensions={0} | all-to-all | bytes 196608 | tf_op jit(solution)/shard_map/edges/all_to_all | solution.py:243
  77.4 0.0 copy-done
  77.4 0.0 copy-done.1
  77.4 0.0 copy-done.2
  77.4 4.0 %lags.1 = bf16[16,64,256]{2,1,0:T(8,128)(2,1)S(1)} custom-call(s32[128]{0:T(128)S(1)} %copy-done, s32[128]{0:T(128)S(1)} %copy-done.1, s32[128]{0:T(128)S(1)} %copy-done.2, bf16[32,72,128]{2,1,0:T(8,128)(2,1)S(1)} %all_to_all.21.refs_3_, bf16[4,96,128]{2,1,0:T(8,128)(2,1)S(1)} %all_to_all.22.refs_4_), custom_call_target="tpu_custom_call" | custom-call | tf_op jit(solution)/shard_map/lags/pallas_call | solution.py:246
  81.4 18.2 %all_to_all.23.got_ref = bf16[16,64,256]{2,1,0:T(8,128)(2,1)} all-to-all(bf16[16,64,256]{2,1,0:T(8,128)(2,1)S(1)} %lags.1), channel_id=1, replica_groups=mesh['y'=4,'zh'=4,'core'=2,'zl'=4,'x'=4] {'zl','x'}, dimensions={0} | all-to-all | bytes 1048576 | tf_op jit(solution)/shard_map/reduce/all_to_all | solution.py:259
  99.6 2.1 %finish.1 = f32[4,16,1024]{2,1,0:T(8,128)} custom-call(bf16[16,64,256]{2,1,0:T(8,128)(2,1)} %all_to_all.23.got_ref), custom_call_target="tpu_custom_call" | custom-call | tf_op jit(solution)/shard_map/finish/pallas_call | solution.py:260
  (6 shorter events, 0.1 us)
Async XLA Ops:
  12.4 0.7 copy-start.3
  66.3 11.1 %copy-start = (s32[128]{0:T(128)S(1)}, s32[128]{0:T(128)}, u32[]{:S(2)}) copy-start(s32[128]{0:T(128)} %refs_0_.1) | copy-start | bytes 1540
  66.3 11.1 %copy-start.1 = (s32[128]{0:T(128)S(1)}, s32[128]{0:T(128)}, u32[]{:S(2)}) copy-start(s32[128]{0:T(128)} %refs_1_.1) | copy-start | bytes 1540
  66.3 11.1 %copy-start.2 = (s32[128]{0:T(128)S(1)}, s32[128]{0:T(128)}, u32[]{:S(2)}) copy-start(s32[128]{0:T(128)} %refs_2_.1) | copy-start | bytes 1540

commit v3 on v2

--- a/solution.py
+++ b/solution.py
@@ -125,13 +125,13 @@
     @pl.when(alive > 0)
     def _():
         lane = lax.broadcasted_iota(jnp.int32, (CB, LANES), 1)
-        zero = jnp.zeros((CB, LANES), jnp.float32)
+        zero = jnp.zeros((CB, LANES), jnp.bfloat16)
         first_scale = scales(edge_ref, 0, first_half, zl, length)
         second_scale = scales(edge_ref, 1, second_half, zl, length)
 
         def white(piece, scale, column):
             shifted = piece.astype(jnp.float32) + scale[:, column + 2 : column + 3]
-            return shifted * scale[:, 0:1]
+            return (shifted * scale[:, 0:1]).astype(jnp.bfloat16)
 
         def first_chunk(chunk):
             return white(data_ref[chunk_place(chunk), :CB], first_scale, chunk // EIGHTHS)
@@ -139,10 +139,10 @@
         def second_chunk(chunk):
             if chunk < 0:
                 piece = white(edge_ref[jnp.maximum(zl - 1, 0), CB : 2 * CB], second_scale, -1)
-                return jnp.where(zl > 0, piece, 0.0)
+                return jnp.where(zl > 0, piece, zero)
             if chunk >= CHUNKS:
                 piece = white(edge_ref[jnp.minimum(zl + 1, ZL - 1), :CB], second_scale, X)
-                return jnp.where(zl < ZL - 1, piece, 0.0)
+                return jnp.where(zl < ZL - 1, piece, zero)
             return white(data_ref[chunk_place(chunk), CB : 2 * CB], second_scale, chunk // EIGHTHS)
 
         here = zero
@@ -153,9 +153,7 @@
                 shift = step * FINE
                 mixed = jnp.where(lane < LANES - shift, here, past)
                 turned = pltpu.roll(mixed, shift, axis=1) if shift else here
-                wide_a[step * CB : (step + 1) * CB, chunk * LANES : (chunk + 1) * LANES] = (
-                    turned.astype(jnp.bfloat16)
-                )
+                wide_a[step * CB : (step + 1) * CB, chunk * LANES : (chunk + 1) * LANES] = turned
         later = second_chunk(-1)
         for chunk in range(-1, CHUNKS + 1):
             here = later
@@ -165,7 +163,7 @@
                 turned = pltpu.roll(mixed, LANES - step, axis=1) if step else here
                 wide_b[
                     step * CB : (step + 1) * CB, (chunk + 1) * LANES : (chunk + 2) * LANES
-                ] = turned.astype(jnp.bfloat16)
+                ] = turned
         for half in range(2):
             result = lax.dot_general(
                 wide_a[...],
@@ -219,6 +217,7 @@
         ),
         in_specs=[VMEM],
         out_specs=(VMEM, VMEM),
+        compiler_params=pltpu.CompilerParams(vmem_limit_bytes=3 * MIB),
         name="split",
     )(samples)
     with jax.named_scope("spread_y"):
@@ -231,6 +230,7 @@
         out_shape=jax.ShapeDtypeStruct((CHUNKS, ROWS, LANES), bf16),
         in_specs=[SMEM, SMEM, VMEM],
         out_specs=VMEM,
+        compiler_params=pltpu.CompilerParams(vmem_limit_bytes=6 * MIB),
         name="select",
     )(tile_rows, tile_offsets, table)
     with jax.named_scope("collect"):
@@ -252,7 +252,7 @@
             pltpu.VMEM((MEDIUM * CB, (CHUNKS + 1) * LANES), bf16),
             pltpu.VMEM((FINE * CB, (CHUNKS + 2) * LANES), bf16),
         ],
-        compiler_params=pltpu.CompilerParams(vmem_limit_bytes=40 * MIB),
+        compiler_params=pltpu.CompilerParams(vmem_limit_bytes=16 * MIB),
         name="lags",
     )(tile_rows, tile_offsets, tile_live, data, edges)
     with jax.named_scope("reduce"):
@@ -266,6 +266,7 @@
             pltpu.VMEM((4 * CB, LANES), jnp.float32),
             pltpu.VMEM((FINE * 8, LANES), jnp.float32),
         ],
+        compiler_params=pltpu.CompilerParams(vmem_limit_bytes=4 * MIB),
         name="finish",
     )(got)
 

time: 102 us -> 95.5 us (0.936)
  the two profiles are of different devices: /device:TPU:32 before, /device:TPU:8 now
where the time goes in v3:
time: 95.5 us; the launch traced here: 95.2 us
  blocking collectives  87.3 us (91%)
  Pallas kernels  6.19 us (6%)
  local copies, waits for them, and re-layouts  1.65 us (2%)
    all_gather x1, blocking collectives, body(): table = lax.all_gather(table, 'zh')  29.2 us
    all_to_all x1, blocking collectives, body(): data = lax.all_to_all(chosen, ('y', 'core', 'x'), 0, 0, tiled=True)  19.2 us
    all_to_all x1, blocking collectives, body(): got = lax.all_to_all(partial, ('zl', 'x'), 0, 0, tiled=True)  17.8 us
    all_to_all x1, blocking collectives, body(): table = lax.all_to_all(parts, ('y', 'core'), 0, 0, tiled=True)  12.9 us
    all_to_all x1, blocking collectives, body(): lax.all_to_all(jnp.broadcast_to(edges[None], (ZL,) + edges.shape), 'zl',...  8.21 us
    pallas_call x1, Pallas kernels, body(): pl.pallas_call(lambda *refs: lag_kernel(length, *refs), out_shape=jax.Sha...  3.74 us

profile of v3, /device:TPU:8, one launch (start us, length us, event | category | flops | bytes accessed | tf_op | source)
XLA Modules:
  0.0 95.2 jit_solution(11610976738693618943)
XLA Ops:
  0.0 0.0 copy-start
  0.0 0.9 copy-done
  1.0 0.3 split.1
  1.2 12.9 %all_to_all.20 = bf16[8,64,128]{2,1,0:T(8,128)(2,1)S(1)} all-to-all(bf16[8,64,128]{2,1,0:T(8,128)(2,1)S(1)} %get-tuple-element.7), channel_id=1, replica_groups=mesh['y'=4,'zh'=4,'core'=2,'zl'=4,'x'=4] {'y','core'}, dimensions={0} | all-to-all | bytes 262144 | tf_op jit(solution)/shard_map/spread_y/all_to_all | solution.py:224
  14.1 29.2 %all-gather = bf16[2080,128]{1,0:T(8,128)(2,1)S(1)} all-gather(bf16[520,128]{1,0:T(8,128)(2,1)S(1)} %pad_maximum_fusion), channel_id=2, replica_groups=mesh['y'=4,'zh'=4,'core'=2,'zl'=4,'x'=4] {'zh'}, dimensions={0}, use_global_device_ids=true | all-gather | bytes 665600 | tf_op jit(solution)/shard_map/spread_z/all_gather | solution.py:227
  43.3 0.0 copy-start.1
  43.3 0.0 copy-start.2
  43.3 0.7 copy-done.1
  44.0 0.0 copy-done.2
  44.0 1.2 %select.1 = bf16[32,72,128]{2,1,0:T(8,128)(2,1)S(1)} custom-call(s32[128]{0:T(128)S(1)} %copy-done.1, s32[128]{0:T(128)S(1)} %copy-done.2, bf16[4,520,128]{2,1,0:T(8,128)(2,1)S(1)} %bitcast.9), custom_call_target="tpu_custom_call" | custom-call | tf_op jit(solution)/shard_map/select/pallas_call | solution.py:228
  45.2 19.2 %all_to_all.21.refs_3_ = bf16[32,72,128]{2,1,0:T(8,128)(2,1)S(1)} all-to-all(bf16[32,72,128]{2,1,0:T(8,128)(2,1)S(1)} %select.1), channel_id=1, replica_groups=mesh['y'=4,'zh'=4,'core'=2,'zl'=4,'x'=4] {'y','core','x'}, dimensions={0} | all-to-all | bytes 1179648 | tf_op jit(solution)/shard_map/collect/all_to_all | solution.py:237
  64.5 0.0 copy-start.3
  64.5 8.2 %all_to_all.22.refs_4_ = bf16[4,96,128]{2,1,0:T(8,128)(2,1)S(1)} all-to-all(bf16[4,96,128]{2,1,0:T(8,128)(2,1)S(1)} %broadcast_in_dim.2), channel_id=1, replica_groups=mesh['y'=4,'zh'=4,'core'=2,'zl'=4,'x'=4] {'zl'}, dimensions={0} | all-to-all | bytes 196608 | tf_op jit(solution)/shard_map/edges/all_to_all | solution.py:243
  72.7 0.0 copy-done.3
  72.7 3.7 %lags.1 = bf16[16,64,256]{2,1,0:T(8,128)(2,1)S(1)} custom-call(s32[128]{0:T(128)S(1)} %copy-done.1, s32[128]{0:T(128)S(1)} %copy-done.2, s32[128]{0:T(128)S(1)} %copy-done.3, bf16[32,72,128]{2,1,0:T(8,128)(2,1)S(1)} %all_to_all.21.refs_3_, bf16[4,96,128]{2,1,0:T(8,128)(2,1)S(1)} %all_to_all.22.refs_4_), custom_call_target="tpu_custom_call" | custom-call | tf_op jit(solution)/shard_map/lags/pallas_call | solution.py:246
  76.5 17.8 %all_to_all.23.got_ref = bf16[16,64,256]{2,1,0:T(8,128)(2,1)S(1)} all-to-all(bf16[16,64,256]{2,1,0:T(8,128)(2,1)S(1)} %lags.1), channel_id=1, replica_groups=mesh['y'=4,'zh'=4,'core'=2,'zl'=4,'x'=4] {'zl','x'}, dimensions={0} | all-to-all | bytes 1048576 | tf_op jit(solution)/shard_map/reduce/all_to_all | solution.py:259
  94.2 1.0 %finish.1 = f32[4,16,1024]{2,1,0:T(8,128)} custom-call(bf16[16,64,256]{2,1,0:T(8,128)(2,1)S(1)} %all_to_all.23.got_ref), custom_call_target="tpu_custom_call" | custom-call | tf_op jit(solution)/shard_map/finish/pallas_call | solution.py:260
  (6 shorter events, 0.1 us)
Async XLA Ops:
  0.0 0.9 copy-start
  43.3 0.7 copy-start.1
  43.3 0.7 copy-start.2
  64.5 8.2 %copy-start.3 = (s32[128]{0:T(128)S(1)}, s32[128]{0:T(128)}, u32[]{:S(2)}) copy-start(s32[128]{0:T(128)} %refs_2_.1) | copy-start | bytes 1540

commit v4 on v3

--- a/solution.py
+++ b/solution.py
@@ -25,6 +25,7 @@
 
 VMEM = pl.BlockSpec(memory_space=pltpu.VMEM)
 SMEM = pl.BlockSpec(memory_space=pltpu.SMEM)
+HBM = pl.BlockSpec(memory_space=pltpu.HBM)
 
 
 def split_kernel(x_ref, out_ref, extra_ref):
@@ -64,48 +65,57 @@
         lines = jnp.where(place == here, lines, jnp.zeros_like(lines))
         return data, lines
 
-    def one(index, carry):
-        place = index >> 2
-        pair = (((place >> 1) * ZH + zh) << 1) | (place & 1)
-        tile = pair * X + (index & (X - 1))
+    for index in range(CHUNKS):
+        place = index // X
+        pair = ((place // CORE * ZH + zh) * CORE) + place % CORE
+        tile = pair * X + index % X
         first = rows_ref[tile]
         data, lines = fetch(first)
         data_second, lines_second = fetch(first + offsets_ref[tile])
         out_ref[index, :CB] = data
         out_ref[index, CB : 2 * CB] = data_second
         out_ref[index, 2 * CB :] = jnp.where(row < EXTRA // 2, lines, lines_second)
-        return carry
-
-    lax.fori_loop(0, EIGHTHS * X, one, 0, unroll=4)
 
 
 def chunk_place(chunk):
     return chunk % EIGHTHS * X + chunk // EIGHTHS
 
 
-def scales(edge_ref, side, half, zl, length):
-    lines = []
+def scales(edge_ref, first_half, second_half, zl, length):
+    row = lax.broadcasted_iota(jnp.int32, (EXTRA, LANES), 0)
+    other = jnp.where(row < EXTRA // 2, first_half, second_half) > 0
+    blocks = []
     for part in range(TMS):
         start = 2 * CB + part % X * EXTRA
-        lines.append(edge_ref[part // X, start : start + EXTRA].astype(jnp.float32))
-    base = side * (EXTRA // 2)
-    sums = [line[base : base + 1] + (line[base + 1 : base + 2] + line[base + 2 : base + 3]) for line in lines]
-    sums = jnp.concatenate(sums, axis=0)
-    sums = jnp.where(half > 0, pltpu.roll(sums, LANES - CB, axis=1), sums)
-    squares = jnp.sum(pltpu.roll(sums, LANES // 2, axis=1), axis=0, keepdims=True)
-    apart = sums - jnp.sum(sums, axis=0, keepdims=True) / TMS
-    power = (squares / length + jnp.sum(apart * apart, axis=0, keepdims=True)) / TMS
+        parts = edge_ref[part // X, start : start + EXTRA].astype(jnp.float32)
+        whole = parts + (pltpu.roll(parts, EXTRA - 1, axis=0) + pltpu.roll(parts, EXTRA - 2, axis=0))
+        blocks.append(jnp.where(other, pltpu.roll(whole, LANES - CB, axis=1), whole))
+    average = sum(blocks[1:], blocks[0]) / TMS
+    squares = pltpu.roll(average, LANES // 2, axis=1)
+    apart = [block - average for block in blocks]
+    spread = [piece * piece for piece in apart]
+    power = squares / length + sum(spread[1:], spread[0]) / TMS
     scaling = lax.rsqrt(power + 1e-05)
-    place = lax.broadcasted_iota(jnp.int32, (TMS, LANES), 0)
-    row = lax.broadcasted_iota(jnp.int32, (8, LANES), 0)
-    packed = jnp.broadcast_to(scaling, (8, LANES))
-    for column in range(X + 2):
-        wanted = zl * X + column - 1
-        one = jnp.sum(jnp.where(place == wanted, apart, 0.0), axis=0, keepdims=True)
-        packed = jnp.where(row == column + 1, one, packed)
-    lane = lax.broadcasted_iota(jnp.int32, (8, LANES), 1)
-    packed = jnp.where(lane < CB, packed, 0.0)
-    return jnp.transpose(jnp.concatenate([packed] * (LANES // 8), axis=0))[:CB, :8]
+
+    def wanted(places):
+        piece = apart[places[0]]
+        for zone in range(1, ZL):
+            piece = jnp.where(zl == zone, apart[places[zone]], piece)
+        return piece
+
+    columns = [scaling, wanted([max(zone * X - 1, 0) for zone in range(ZL)])]
+    columns += [wanted([zone * X + x for zone in range(ZL)]) for x in range(X)]
+    columns.append(wanted([min(zone * X + X, TMS - 1) for zone in range(ZL)]))
+    lane = lax.broadcasted_iota(jnp.int32, (EXTRA, LANES), 1)
+    turned = []
+    for base in (0, EXTRA // 2):
+        packed = jnp.zeros((EXTRA, LANES), jnp.float32)
+        for place, column in enumerate(columns):
+            packed = jnp.where(row == place, column[base : base + 1], packed)
+        turned.append(jnp.where(lane < CB, packed, 0.0))
+    filler = jnp.zeros((LANES - 2 * EXTRA, LANES), jnp.float32)
+    turned = jnp.transpose(jnp.concatenate(turned + [filler], axis=0))
+    return turned[:CB, :EXTRA], turned[:CB, EXTRA : 2 * EXTRA]
 
 
 def lag_kernel(length, rows_ref, offsets_ref, live_ref, data_ref, edge_ref, out_ref, wide_a, wide_b):
@@ -126,8 +136,7 @@
     def _():
         lane = lax.broadcasted_iota(jnp.int32, (CB, LANES), 1)
         zero = jnp.zeros((CB, LANES), jnp.bfloat16)
-        first_scale = scales(edge_ref, 0, first_half, zl, length)
-        second_scale = scales(edge_ref, 1, second_half, zl, length)
+        first_scale, second_scale = scales(edge_ref, first_half, second_half, zl, length)
 
         def white(piece, scale, column):
             shifted = piece.astype(jnp.float32) + scale[:, column + 2 : column + 3]
@@ -176,8 +185,9 @@
                 out_ref[half * (TMS // 2) + part] = rounded[part * 2 * CB : (part + 1) * 2 * CB]
 
 
-def finish_kernel(got_ref, out_ref, grid_ref, turn_ref):
+def finish_kernel(got_ref, out_hbm, out_ref, grid_ref, turn_ref, sems):
     lane = lax.broadcasted_iota(jnp.int32, (8, LANES), 1)
+    copies = []
     for slot in range(X):
         total = got_ref[slot].astype(jnp.float32)
         for zl in range(1, ZL):
@@ -204,6 +214,10 @@
                 out_ref[slot, half * 8 : half * 8 + 8, k * LANES : (k + 1) * LANES] = turn_ref[
                     pl.ds(k, 8, stride=8), :
                 ]
+        copies.append(pltpu.make_async_copy(out_ref.at[slot], out_hbm.at[slot], sems.at[slot]))
+        copies[-1].start()
+    for copy in copies:
+        copy.wait()
 
 
 def body(samples, tile_rows, tile_offsets, tile_live):
@@ -261,10 +275,12 @@
         finish_kernel,
         out_shape=jax.ShapeDtypeStruct((X, 2 * FINE, CB * CB), jnp.float32),
         in_specs=[VMEM],
-        out_specs=VMEM,
+        out_specs=HBM,
         scratch_shapes=[
+            pltpu.VMEM((X, 2 * FINE, CB * CB), jnp.float32),
             pltpu.VMEM((4 * CB, LANES), jnp.float32),
             pltpu.VMEM((FINE * 8, LANES), jnp.float32),
+            pltpu.SemaphoreType.DMA((X,)),
         ],
         compiler_params=pltpu.CompilerParams(vmem_limit_bytes=4 * MIB),
         name="finish",

time: 95.5 us -> 96.1 us (level)
  the two profiles are of different devices: /device:TPU:8 before, /device:TPU:32 now
where the time goes in v4:
time: 96.1 us; the launch traced here: 95.9 us
  blocking collectives  88.2 us (92%)
  Pallas kernels  5.94 us (6%)
  local copies, waits for them, and re-layouts  1.65 us (2%)
    all_gather x1, blocking collectives, body(): table = lax.all_gather(table, 'zh')  32.4 us
    all_to_all x1, blocking collectives, body(): got = lax.all_to_all(partial, ('zl', 'x'), 0, 0, tiled=True)  18.6 us
    all_to_all x1, blocking collectives, body(): data = lax.all_to_all(chosen, ('y', 'core', 'x'), 0, 0, tiled=True)  17.5 us
    all_to_all x1, blocking collectives, body(): table = lax.all_to_all(parts, ('y', 'core'), 0, 0, tiled=True)  10.4 us
    all_to_all x1, blocking collectives, body(): lax.all_to_all(jnp.broadcast_to(edges[None], (ZL,) + edges.shape), 'zl',...  9.16 us
    pallas_call x1, Pallas kernels, body(): pl.pallas_call(lambda *refs: lag_kernel(length, *refs), out_shape=jax.Sha...  3.66 us

profile of v4, /device:TPU:32, one launch (start us, length us, event | category | flops | bytes accessed | tf_op | source)
XLA Modules:
  0.0 95.9 jit_solution(13144529939389844111)
XLA Ops:
  0.0 0.0 copy-start
  0.0 0.9 copy-done
  1.0 0.3 split.1
  1.2 10.4 %all_to_all.20 = bf16[8,64,128]{2,1,0:T(8,128)(2,1)S(1)} all-to-all(bf16[8,64,128]{2,1,0:T(8,128)(2,1)S(1)} %get-tuple-element.7), channel_id=1, replica_groups=mesh['y'=4,'zh'=4,'core'=2,'zl'=4,'x'=4] {'y','core'}, dimensions={0} | all-to-all | bytes 262144 | tf_op jit(solution)/shard_map/spread_y/all_to_all | solution.py:238
  11.7 32.4 %all-gather = bf16[2080,128]{1,0:T(8,128)(2,1)S(1)} all-gather(bf16[520,128]{1,0:T(8,128)(2,1)S(1)} %pad_maximum_fusion), channel_id=2, replica_groups=mesh['y'=4,'zh'=4,'core'=2,'zl'=4,'x'=4] {'zh'}, dimensions={0}, use_global_device_ids=true | all-gather | bytes 665600 | tf_op jit(solution)/shard_map/spread_z/all_gather | solution.py:241
  44.1 0.0 copy-start.1
  44.1 0.0 copy-start.2
  44.1 0.7 copy-done.1
  44.7 0.0 copy-done.2
  44.8 1.0 %select.1 = bf16[32,72,128]{2,1,0:T(8,128)(2,1)S(1)} custom-call(s32[128]{0:T(128)S(1)} %copy-done.1, s32[128]{0:T(128)S(1)} %copy-done.2, bf16[4,520,128]{2,1,0:T(8,128)(2,1)S(1)} %bitcast.9), custom_call_target="tpu_custom_call" | custom-call | tf_op jit(solution)/shard_map/select/pallas_call | solution.py:242
  45.8 17.5 %all_to_all.21.refs_3_ = bf16[32,72,128]{2,1,0:T(8,128)(2,1)S(1)} all-to-all(bf16[32,72,128]{2,1,0:T(8,128)(2,1)S(1)} %select.1), channel_id=1, replica_groups=mesh['y'=4,'zh'=4,'core'=2,'zl'=4,'x'=4] {'y','core','x'}, dimensions={0} | all-to-all | bytes 1179648 | tf_op jit(solution)/shard_map/collect/all_to_all | solution.py:251
  63.4 0.0 copy-start.3
  63.4 9.2 %all_to_all.22.refs_4_ = bf16[4,96,128]{2,1,0:T(8,128)(2,1)S(1)} all-to-all(bf16[4,96,128]{2,1,0:T(8,128)(2,1)S(1)} %broadcast_in_dim.2), channel_id=1, replica_groups=mesh['y'=4,'zh'=4,'core'=2,'zl'=4,'x'=4] {'zl'}, dimensions={0} | all-to-all | bytes 196608 | tf_op jit(solution)/shard_map/edges/all_to_all | solution.py:257
  72.6 0.0 copy-done.3
  72.6 3.7 %lags.1 = bf16[16,64,256]{2,1,0:T(8,128)(2,1)S(1)} custom-call(s32[128]{0:T(128)S(1)} %copy-done.1, s32[128]{0:T(128)S(1)} %copy-done.2, s32[128]{0:T(128)S(1)} %copy-done.3, bf16[32,72,128]{2,1,0:T(8,128)(2,1)S(1)} %all_to_all.21.refs_3_, bf16[4,96,128]{2,1,0:T(8,128)(2,1)S(1)} %all_to_all.22.refs_4_), custom_call_target="tpu_custom_call" | custom-call | tf_op jit(solution)/shard_map/lags/pallas_call | solution.py:260
  76.2 18.6 %all_to_all.23.got_ref = bf16[16,64,256]{2,1,0:T(8,128)(2,1)S(1)} all-to-all(bf16[16,64,256]{2,1,0:T(8,128)(2,1)S(1)} %lags.1), channel_id=1, replica_groups=mesh['y'=4,'zh'=4,'core'=2,'zl'=4,'x'=4] {'zl','x'}, dimensions={0} | all-to-all | bytes 1048576 | tf_op jit(solution)/shard_map/reduce/all_to_all | solution.py:273
  94.9 1.0 %finish.1 = f32[4,16,1024]{2,1,0:T(8,128)} custom-call(bf16[16,64,256]{2,1,0:T(8,128)(2,1)S(1)} %all_to_all.23.got_ref), custom_call_target="tpu_custom_call" | custom-call | tf_op jit(solution)/shard_map/finish/pallas_call | solution.py:274
  (6 shorter events, 0.1 us)
Async XLA Ops:
  0.0 0.9 copy-start
  44.1 0.7 copy-start.1
  44.1 0.7 copy-start.2
  63.4 9.2 %copy-start.3 = (s32[128]{0:T(128)S(1)}, s32[128]{0:T(128)}, u32[]{:S(2)}) copy-start(s32[128]{0:T(128)} %refs_2_.1) | copy-start | bytes 1540

commit v5 on v4

--- a/solution.py
+++ b/solution.py
@@ -28,8 +28,14 @@
 HBM = pl.BlockSpec(memory_space=pltpu.HBM)
 
 
-def split_kernel(x_ref, out_ref, extra_ref):
+def split_kernel(x_hbm, rows_hbm, offsets_hbm, live_hbm, out_ref, extra_ref, plan_ref, x_ref, sems):
     rows, length = x_ref.shape
+    copies = [pltpu.make_async_copy(x_hbm, x_ref, sems.at[0])]
+    for place, ref in enumerate((rows_hbm, offsets_hbm, live_hbm)):
+        copies.append(pltpu.make_async_copy(ref, plan_ref.at[place], sems.at[place + 1]))
+    for copy in copies:
+        copy.start()
+    copies[0].wait()
     mean = jnp.sum(x_ref[...], axis=1, keepdims=True) / length
     spread = jnp.zeros((rows, 1), jnp.float32)
     for part in range(EIGHTHS):
@@ -47,9 +53,11 @@
     row = lax.broadcasted_iota(jnp.int32, (EXTRA, LANES), 0) % (EXTRA // 2)
     lines = jnp.where(row == 0, high, jnp.where(row == 1, middle, jnp.where(row == 2, low, 0.0)))
     extra_ref[...] = lines.astype(jnp.bfloat16)
-
-
-def select_kernel(rows_ref, offsets_ref, table_ref, out_ref):
+    for copy in copies[1:]:
+        copy.wait()
+
+
+def select_kernel(plan_ref, table_ref, out_ref):
     zh = lax.axis_index("zh")
     here = lax.axis_index("y") * CORE + lax.axis_index("core")
     bulk = EIGHTHS * 2 * CB
@@ -69,9 +77,9 @@
         place = index // X
         pair = ((place // CORE * ZH + zh) * CORE) + place % CORE
         tile = pair * X + index % X
-        first = rows_ref[tile]
+        first = plan_ref[0, 0, tile]
         data, lines = fetch(first)
-        data_second, lines_second = fetch(first + offsets_ref[tile])
+        data_second, lines_second = fetch(first + plan_ref[1, 0, tile])
         out_ref[index, :CB] = data
         out_ref[index, CB : 2 * CB] = data_second
         out_ref[index, 2 * CB :] = jnp.where(row < EXTRA // 2, lines, lines_second)
@@ -118,13 +126,13 @@
     return turned[:CB, :EXTRA], turned[:CB, EXTRA : 2 * EXTRA]
 
 
-def lag_kernel(length, rows_ref, offsets_ref, live_ref, data_ref, edge_ref, out_ref, wide_a, wide_b):
+def lag_kernel(length, plan_ref, data_ref, edge_ref, out_ref, wide_a, wide_b):
     zl = lax.axis_index("zl")
     pair = (lax.axis_index("y") * ZH + lax.axis_index("zh")) * CORE + lax.axis_index("core")
     tile = pair * X + lax.axis_index("x")
-    alive = live_ref[tile]
-    first_half = lax.rem(rows_ref[tile], 2)
-    second_half = lax.rem(rows_ref[tile] + offsets_ref[tile] + PAIRS * 2, 2)
+    alive = plan_ref[2, 0, tile]
+    first_half = plan_ref[0, 0, tile] & 1
+    second_half = (plan_ref[0, 0, tile] + plan_ref[1, 0, tile]) & 1
     width = (CHUNKS + 1) * LANES
     factor = 1.0 / math.sqrt(length * TMS)
 
@@ -223,17 +231,27 @@
 def body(samples, tile_rows, tile_offsets, tile_live):
     length = samples.shape[1]
     bf16 = jnp.bfloat16
-    parts, lines = pl.pallas_call(
+    parts, lines, plan = pl.pallas_call(
         split_kernel,
         out_shape=(
             jax.ShapeDtypeStruct((EIGHTHS, 2 * CB, LANES), bf16),
             jax.ShapeDtypeStruct((EXTRA, LANES), bf16),
+            jax.ShapeDtypeStruct((3, 1, LANES), jnp.int32),
         ),
-        in_specs=[VMEM],
-        out_specs=(VMEM, VMEM),
+        in_specs=[HBM] * 4,
+        out_specs=(VMEM, VMEM, VMEM),
+        scratch_shapes=[
+            pltpu.VMEM(samples.shape, jnp.float32),
+            pltpu.SemaphoreType.DMA((4,)),
+        ],
         compiler_params=pltpu.CompilerParams(vmem_limit_bytes=3 * MIB),
         name="split",
-    )(samples)
+    )(
+        *(
+            pltpu.with_memory_space_constraint(array, pltpu.HBM)
+            for array in (samples, tile_rows[None], tile_offsets[None], tile_live[None])
+        )
+    )
     with jax.named_scope("spread_y"):
         table = lax.all_to_all(parts, ("y", "core"), 0, 0, tiled=True)
     with jax.named_scope("spread_z"):
@@ -242,11 +260,11 @@
     chosen = pl.pallas_call(
         select_kernel,
         out_shape=jax.ShapeDtypeStruct((CHUNKS, ROWS, LANES), bf16),
-        in_specs=[SMEM, SMEM, VMEM],
+        in_specs=[SMEM, VMEM],
         out_specs=VMEM,
         compiler_params=pltpu.CompilerParams(vmem_limit_bytes=6 * MIB),
         name="select",
-    )(tile_rows, tile_offsets, table)
+    )(plan, table)
     with jax.named_scope("collect"):
         data = lax.all_to_all(chosen, ("y", "core", "x"), 0, 0, tiled=True)
     with jax.named_scope("edges"):
@@ -260,7 +278,7 @@
     partial = pl.pallas_call(
         lambda *refs: lag_kernel(length, *refs),
         out_shape=jax.ShapeDtypeStruct((TMS, 2 * CB, FINE * CB), bf16),
-        in_specs=[SMEM, SMEM, SMEM, VMEM, VMEM],
+        in_specs=[SMEM, VMEM, VMEM],
         out_specs=VMEM,
         scratch_shapes=[
             pltpu.VMEM((MEDIUM * CB, (CHUNKS + 1) * LANES), bf16),
@@ -268,7 +286,7 @@
         ],
         compiler_params=pltpu.CompilerParams(vmem_limit_bytes=16 * MIB),
         name="lags",
-    )(tile_rows, tile_offsets, tile_live, data, edges)
+    )(plan, data, edges)
     with jax.named_scope("reduce"):
         got = lax.all_to_all(partial, ("zl", "x"), 0, 0, tiled=True)
     return pl.pallas_call(

time: 96.1 us -> 95.6 us (level)
  local copies, waits for them, and re-layouts: 1.65 us -> 0.02 us
  Pallas kernels: 5.94 us -> 7.01 us
    unnamed x8 -> x0, local copies, waits for them, and re-layouts: 1.63 us -> none
    pallas_call x1, Pallas kernels: 0.28 us -> 1.28 us  [body(): pl.pallas_call(split_kernel, out_shape=(jax.ShapeDtypeStruct((EIGHTHS, 2...]
where the time goes in v5:
time: 95.6 us; the launch traced here: 95.3 us
  blocking collectives  88.2 us (92%)
  Pallas kernels  7.01 us (7%)
    all_gather x1, blocking collectives, body(): table = lax.all_gather(table, 'zh')  32.4 us
    all_to_all x1, blocking collectives, body(): got = lax.all_to_all(partial, ('zl', 'x'), 0, 0, tiled=True)  18.6 us
    all_to_all x1, blocking collectives, body(): data = lax.all_to_all(chosen, ('y', 'core', 'x'), 0, 0, tiled=True)  17.5 us
    all_to_all x1, blocking collectives, body(): table = lax.all_to_all(parts, ('y', 'core'), 0, 0, tiled=True)  10.4 us
    all_to_all x1, blocking collectives, body(): lax.all_to_all(jnp.broadcast_to(edges[None], (ZL,) + edges.shape), 'zl',...  9.16 us
    pallas_call x1, Pallas kernels, body(): pl.pallas_call(lambda *refs: lag_kernel(length, *refs), out_shape=jax.Sha...  3.67 us

profile of v5, /device:TPU:32, one launch (start us, length us, event | category | flops | bytes accessed | tf_op | source)
XLA Modules:
  0.0 95.3 jit_solution(18068095872087941215)
XLA Ops:
  0.0 1.3 %split.1 = (bf16[8,64,128]{2,1,0:T(8,128)(2,1)S(1)}, bf16[8,128]{1,0:T(8,128)(2,1)S(1)}, s32[3,1,128]{2,1,0:T(1,128)S(1)}) custom-call(f32[64,1024]{1,0:T(8,128)} %x_hbm.1, s32[1,128]{1,0:T(1,128)} %bitcast.15, s32[1,128]{1,0:T(1,128)} %bitcast.16, s32[1,128]{1,0:T(1,128)} %bitcast.17), custom_call_target="tpu_custom_call" | custom-call | tf_op jit(solution)/shard_map/split/pallas_call | solution.py:234
  1.3 10.4 %all_to_all.20 = bf16[8,64,128]{2,1,0:T(8,128)(2,1)S(1)} all-to-all(bf16[8,64,128]{2,1,0:T(8,128)(2,1)S(1)} %get-tuple-element.9), channel_id=1, replica_groups=mesh['y'=4,'zh'=4,'core'=2,'zl'=4,'x'=4] {'y','core'}, dimensions={0} | all-to-all | bytes 262144 | tf_op jit(solution)/shard_map/spread_y/all_to_all | solution.py:256
  11.7 32.4 %all-gather = bf16[2080,128]{1,0:T(8,128)(2,1)S(1)} all-gather(bf16[520,128]{1,0:T(8,128)(2,1)S(1)} %pad_maximum_fusion), channel_id=2, replica_groups=mesh['y'=4,'zh'=4,'core'=2,'zl'=4,'x'=4] {'zh'}, dimensions={0}, use_global_device_ids=true | all-gather | bytes 665600 | tf_op jit(solution)/shard_map/spread_z/all_gather | solution.py:259
  44.1 1.1 %select.1 = bf16[32,72,128]{2,1,0:T(8,128)(2,1)S(1)} custom-call(s32[3,1,128]{2,1,0:T(1,128)S(1)} %get-tuple-element.8.plan_ref.refs_0_, bf16[4,520,128]{2,1,0:T(8,128)(2,1)S(1)} %bitcast.12), custom_call_target="tpu_custom_call" | custom-call | tf_op jit(solution)/shard_map/select/pallas_call | solution.py:260
  45.2 17.5 %all_to_all.21.refs_1_ = bf16[32,72,128]{2,1,0:T(8,128)(2,1)S(1)} all-to-all(bf16[32,72,128]{2,1,0:T(8,128)(2,1)S(1)} %select.1), channel_id=1, replica_groups=mesh['y'=4,'zh'=4,'core'=2,'zl'=4,'x'=4] {'y','core','x'}, dimensions={0} | all-to-all | bytes 1179648 | tf_op jit(solution)/shard_map/collect/all_to_all | solution.py:269
  62.8 9.2 %all_to_all.22.refs_2_ = bf16[4,96,128]{2,1,0:T(8,128)(2,1)S(1)} all-to-all(bf16[4,96,128]{2,1,0:T(8,128)(2,1)S(1)} %broadcast_in_dim.18), channel_id=1, replica_groups=mesh['y'=4,'zh'=4,'core'=2,'zl'=4,'x'=4] {'zl'}, dimensions={0} | all-to-all | bytes 196608 | tf_op jit(solution)/shard_map/edges/all_to_all | solution.py:275
  72.0 3.7 %lags.1 = bf16[16,64,256]{2,1,0:T(8,128)(2,1)S(1)} custom-call(s32[3,1,128]{2,1,0:T(1,128)S(1)} %get-tuple-element.8.plan_ref.refs_0_, bf16[32,72,128]{2,1,0:T(8,128)(2,1)S(1)} %all_to_all.21.refs_1_, bf16[4,96,128]{2,1,0:T(8,128)(2,1)S(1)} %all_to_all.22.refs_2_), custom_call_target="tpu_custom_call" | custom-call | tf_op jit(solution)/shard_map/lags/pallas_call | solution.py:278
  75.7 18.6 %all_to_all.23.got_ref = bf16[16,64,256]{2,1,0:T(8,128)(2,1)S(1)} all-to-all(bf16[16,64,256]{2,1,0:T(8,128)(2,1)S(1)} %lags.1), channel_id=1, replica_groups=mesh['y'=4,'zh'=4,'core'=2,'zl'=4,'x'=4] {'zl','x'}, dimensions={0} | all-to-all | bytes 1048576 | tf_op jit(solution)/shard_map/reduce/all_to_all | solution.py:291
  94.3 1.0 %finish.1 = f32[4,16,1024]{2,1,0:T(8,128)} custom-call(bf16[16,64,256]{2,1,0:T(8,128)(2,1)S(1)} %all_to_all.23.got_ref), custom_call_target="tpu_custom_call" | custom-call | tf_op jit(solution)/shard_map/finish/pallas_call | solution.py:292
  (6 shorter events, 0.1 us)

commit v6 on v5

--- a/solution.py
+++ b/solution.py
@@ -236,10 +236,10 @@
         out_shape=(
             jax.ShapeDtypeStruct((EIGHTHS, 2 * CB, LANES), bf16),
             jax.ShapeDtypeStruct((EXTRA, LANES), bf16),
-            jax.ShapeDtypeStruct((3, 1, LANES), jnp.int32),
+            pltpu.SMEM((3, 1, LANES), jnp.int32),
         ),
         in_specs=[HBM] * 4,
-        out_specs=(VMEM, VMEM, VMEM),
+        out_specs=(VMEM, VMEM, SMEM),
         scratch_shapes=[
             pltpu.VMEM(samples.shape, jnp.float32),
             pltpu.SemaphoreType.DMA((4,)),
@@ -264,7 +264,7 @@
         out_specs=VMEM,
         compiler_params=pltpu.CompilerParams(vmem_limit_bytes=6 * MIB),
         name="select",
-    )(plan, table)
+    )(pltpu.with_memory_space_constraint(plan, pltpu.SMEM), table)
     with jax.named_scope("collect"):
         data = lax.all_to_all(chosen, ("y", "core", "x"), 0, 0, tiled=True)
     with jax.named_scope("edges"):
@@ -286,7 +286,7 @@
         ],
         compiler_params=pltpu.CompilerParams(vmem_limit_bytes=16 * MIB),
         name="lags",
-    )(plan, data, edges)
+    )(pltpu.with_memory_space_constraint(plan, pltpu.SMEM), data, edges)
     with jax.named_scope("reduce"):
         got = lax.all_to_all(partial, ("zl", "x"), 0, 0, tiled=True)
     return pl.pallas_call(

time: 95.6 us -> 94.3 us (0.986)
  Pallas kernels: 7.01 us -> 5.85 us
where the time goes in v6:
time: 94.3 us; the launch traced here: 94 us
  blocking collectives  88.1 us (93%)
  Pallas kernels  5.85 us (6%)
    all_gather x1, blocking collectives, body(): table = lax.all_gather(table, 'zh')  32.4 us
    all_to_all x1, blocking collectives, body(): got = lax.all_to_all(partial, ('zl', 'x'), 0, 0, tiled=True)  18.6 us
    all_to_all x1, blocking collectives, body(): data = lax.all_to_all(chosen, ('y', 'core', 'x'), 0, 0, tiled=True)  17.5 us
    all_to_all x1, blocking collectives, body(): table = lax.all_to_all(parts, ('y', 'core'), 0, 0, tiled=True)  10.4 us
    all_to_all x1, blocking collectives, body(): lax.all_to_all(jnp.broadcast_to(edges[None], (ZL,) + edges.shape), 'zl',...  9.16 us
    pallas_call x1, Pallas kernels, body(): pl.pallas_call(lambda *refs: lag_kernel(length, *refs), out_shape=jax.Sha...  3.07 us

profile of v6, /device:TPU:32, one launch (start us, length us, event | category | flops | bytes accessed | tf_op | source)
XLA Modules:
  0.0 94.0 jit_solution(8884739451395514424)
XLA Ops:
  0.0 1.3 %split.1 = (bf16[8,64,128]{2,1,0:T(8,128)(2,1)S(1)}, bf16[8,128]{1,0:T(8,128)(2,1)S(1)}, s32[3,1,128]{2,1,0:T(1,128)S(4)}) custom-call(f32[64,1024]{1,0:T(8,128)} %x_hbm.1, s32[1,128]{1,0:T(1,128)} %bitcast.15, s32[1,128]{1,0:T(1,128)} %bitcast.16, s32[1,128]{1,0:T(1,128)} %bitcast.17), custom_call_target="tpu_custom_call" | custom-call | tf_op jit(solution)/shard_map/split/pallas_call | solution.py:234
  1.3 10.4 %all_to_all.20 = bf16[8,64,128]{2,1,0:T(8,128)(2,1)S(1)} all-to-all(bf16[8,64,128]{2,1,0:T(8,128)(2,1)S(1)} %get-tuple-element.9), channel_id=1, replica_groups=mesh['y'=4,'zh'=4,'core'=2,'zl'=4,'x'=4] {'y','core'}, dimensions={0} | all-to-all | bytes 262144 | tf_op jit(solution)/shard_map/spread_y/all_to_all | solution.py:256
  11.7 32.4 %all-gather = bf16[2080,128]{1,0:T(8,128)(2,1)S(1)} all-gather(bf16[520,128]{1,0:T(8,128)(2,1)S(1)} %pad_maximum_fusion), channel_id=2, replica_groups=mesh['y'=4,'zh'=4,'core'=2,'zl'=4,'x'=4] {'zh'}, dimensions={0}, use_global_device_ids=true | all-gather | bytes 665600 | tf_op jit(solution)/shard_map/spread_z/all_gather | solution.py:259
  44.2 0.5 select.1
  44.7 17.5 %all_to_all.21.refs_1_ = bf16[32,72,128]{2,1,0:T(8,128)(2,1)S(1)} all-to-all(bf16[32,72,128]{2,1,0:T(8,128)(2,1)S(1)} %select.1), channel_id=1, replica_groups=mesh['y'=4,'zh'=4,'core'=2,'zl'=4,'x'=4] {'y','core','x'}, dimensions={0} | all-to-all | bytes 1179648 | tf_op jit(solution)/shard_map/collect/all_to_all | solution.py:269
  62.3 9.2 %all_to_all.22.refs_2_ = bf16[4,96,128]{2,1,0:T(8,128)(2,1)S(1)} all-to-all(bf16[4,96,128]{2,1,0:T(8,128)(2,1)S(1)} %broadcast_in_dim.18), channel_id=1, replica_groups=mesh['y'=4,'zh'=4,'core'=2,'zl'=4,'x'=4] {'zl'}, dimensions={0} | all-to-all | bytes 196608 | tf_op jit(solution)/shard_map/edges/all_to_all | solution.py:275
  71.4 3.1 %lags.1 = bf16[16,64,256]{2,1,0:T(8,128)(2,1)S(1)} custom-call(s32[3,1,128]{2,1,0:T(1,128)S(4)} %get-tuple-element.8.plan_ref.refs_0_, bf16[32,72,128]{2,1,0:T(8,128)(2,1)S(1)} %all_to_all.21.refs_1_, bf16[4,96,128]{2,1,0:T(8,128)(2,1)S(1)} %all_to_all.22.refs_2_), custom_call_target="tpu_custom_call" | custom-call | tf_op jit(solution)/shard_map/lags/pallas_call | solution.py:278
  74.5 18.6 %all_to_all.23.got_ref = bf16[16,64,256]{2,1,0:T(8,128)(2,1)S(1)} all-to-all(bf16[16,64,256]{2,1,0:T(8,128)(2,1)S(1)} %lags.1), channel_id=1, replica_groups=mesh['y'=4,'zh'=4,'core'=2,'zl'=4,'x'=4] {'zl','x'}, dimensions={0} | all-to-all | bytes 1048576 | tf_op jit(solution)/shard_map/reduce/all_to_all | solution.py:291
  93.1 1.0 %finish.1 = f32[4,16,1024]{2,1,0:T(8,128)} custom-call(bf16[16,64,256]{2,1,0:T(8,128)(2,1)S(1)} %all_to_all.23.got_ref), custom_call_target="tpu_custom_call" | custom-call | tf_op jit(solution)/shard_map/finish/pallas_call | solution.py:292
  (6 shorter events, 0.1 us)

commit v7 on v6

--- a/solution.py
+++ b/solution.py
@@ -43,10 +43,9 @@
         spread = spread + jnp.sum(piece * piece, axis=1, keepdims=True)
         out_ref[part] = piece.astype(jnp.bfloat16)
     lane = lax.broadcasted_iota(jnp.int32, (rows, LANES), 1)
-    columns = jnp.where(lane == 0, mean, jnp.where(lane == 1, spread, 0.0))
-    turned = jnp.transpose(jnp.concatenate([columns] * (LANES // rows), axis=0))
-    wide = lax.broadcasted_iota(jnp.int32, (1, LANES), 1)
-    line = jnp.where(wide < rows, turned[0:1], turned[1:2])
+    channel = lax.broadcasted_iota(jnp.int32, (rows, LANES), 0)
+    placed = jnp.where(lane == channel, mean, jnp.where(lane == channel + rows, spread, 0.0))
+    line = jnp.sum(placed, axis=0, keepdims=True)
     high = line.astype(jnp.bfloat16).astype(jnp.float32)
     middle = (line - high).astype(jnp.bfloat16).astype(jnp.float32)
     low = line - high - middle
@@ -193,9 +192,8 @@
                 out_ref[half * (TMS // 2) + part] = rounded[part * 2 * CB : (part + 1) * 2 * CB]
 
 
-def finish_kernel(got_ref, out_hbm, out_ref, grid_ref, turn_ref, sems):
+def finish_kernel(got_ref, out_hbm, out_ref, grid_ref, turn_ref, sem):
     lane = lax.broadcasted_iota(jnp.int32, (8, LANES), 1)
-    copies = []
     for slot in range(X):
         total = got_ref[slot].astype(jnp.float32)
         for zl in range(1, ZL):
@@ -222,10 +220,9 @@
                 out_ref[slot, half * 8 : half * 8 + 8, k * LANES : (k + 1) * LANES] = turn_ref[
                     pl.ds(k, 8, stride=8), :
                 ]
-        copies.append(pltpu.make_async_copy(out_ref.at[slot], out_hbm.at[slot], sems.at[slot]))
-        copies[-1].start()
-    for copy in copies:
-        copy.wait()
+    copy = pltpu.make_async_copy(out_ref, out_hbm, sem)
+    copy.start()
+    copy.wait()
 
 
 def body(samples, tile_rows, tile_offsets, tile_live):
@@ -298,7 +295,7 @@
             pltpu.VMEM((X, 2 * FINE, CB * CB), jnp.float32),
             pltpu.VMEM((4 * CB, LANES), jnp.float32),
             pltpu.VMEM((FINE * 8, LANES), jnp.float32),
-            pltpu.SemaphoreType.DMA((X,)),
+            pltpu.SemaphoreType.DMA,
         ],
         compiler_params=pltpu.CompilerParams(vmem_limit_bytes=4 * MIB),
         name="finish",

time: 94.3 us -> 94.4 us (level)
  no operation moved by 1% of the time
where the time goes in v7:
time: 94.4 us; the launch traced here: 94.1 us
  blocking collectives  88.2 us (93%)
  Pallas kernels  5.85 us (6%)
    all_gather x1, blocking collectives, body(): table = lax.all_gather(table, 'zh')  32.4 us
    all_to_all x1, blocking collectives, body(): got = lax.all_to_all(partial, ('zl', 'x'), 0, 0, tiled=True)  18.6 us
    all_to_all x1, blocking collectives, body(): data = lax.all_to_all(chosen, ('y', 'core', 'x'), 0, 0, tiled=True)  17.5 us
    all_to_all x1, blocking collectives, body(): table = lax.all_to_all(parts, ('y', 'core'), 0, 0, tiled=True)  10.4 us
    all_to_all x1, blocking collectives, body(): lax.all_to_all(jnp.broadcast_to(edges[None], (ZL,) + edges.shape), 'zl',...  9.16 us
    pallas_call x1, Pallas kernels, body(): pl.pallas_call(lambda *refs: lag_kernel(length, *refs), out_shape=jax.Sha...  3.07 us

profile of v7, /device:TPU:32, one launch (start us, length us, event | category | flops | bytes accessed | tf_op | source)
XLA Modules:
  0.0 94.1 jit_solution(15325666716294782064)
XLA Ops:
  0.0 1.3 %split.1 = (bf16[8,64,128]{2,1,0:T(8,128)(2,1)S(1)}, bf16[8,128]{1,0:T(8,128)(2,1)S(1)}, s32[3,1,128]{2,1,0:T(1,128)S(4)}) custom-call(f32[64,1024]{1,0:T(8,128)} %x_hbm.1, s32[1,128]{1,0:T(1,128)} %bitcast.15, s32[1,128]{1,0:T(1,128)} %bitcast.16, s32[1,128]{1,0:T(1,128)} %bitcast.17), custom_call_target="tpu_custom_call" | custom-call | tf_op jit(solution)/shard_map/split/pallas_call | solution.py:231
  1.3 10.4 %all_to_all.20 = bf16[8,64,128]{2,1,0:T(8,128)(2,1)S(1)} all-to-all(bf16[8,64,128]{2,1,0:T(8,128)(2,1)S(1)} %get-tuple-element.9), channel_id=1, replica_groups=mesh['y'=4,'zh'=4,'core'=2,'zl'=4,'x'=4] {'y','core'}, dimensions={0} | all-to-all | bytes 262144 | tf_op jit(solution)/shard_map/spread_y/all_to_all | solution.py:253
  11.7 32.4 %all-gather = bf16[2080,128]{1,0:T(8,128)(2,1)S(1)} all-gather(bf16[520,128]{1,0:T(8,128)(2,1)S(1)} %pad_maximum_fusion), channel_id=2, replica_groups=mesh['y'=4,'zh'=4,'core'=2,'zl'=4,'x'=4] {'zh'}, dimensions={0}, use_global_device_ids=true | all-gather | bytes 665600 | tf_op jit(solution)/shard_map/spread_z/all_gather | solution.py:256
  44.1 0.5 select.1
  44.6 17.5 %all_to_all.21.refs_1_ = bf16[32,72,128]{2,1,0:T(8,128)(2,1)S(1)} all-to-all(bf16[32,72,128]{2,1,0:T(8,128)(2,1)S(1)} %select.1), channel_id=1, replica_groups=mesh['y'=4,'zh'=4,'core'=2,'zl'=4,'x'=4] {'y','core','x'}, dimensions={0} | all-to-all | bytes 1179648 | tf_op jit(solution)/shard_map/collect/all_to_all | solution.py:266
  62.2 9.2 %all_to_all.22.refs_2_ = bf16[4,96,128]{2,1,0:T(8,128)(2,1)S(1)} all-to-all(bf16[4,96,128]{2,1,0:T(8,128)(2,1)S(1)} %broadcast_in_dim.18), channel_id=1, replica_groups=mesh['y'=4,'zh'=4,'core'=2,'zl'=4,'x'=4] {'zl'}, dimensions={0} | all-to-all | bytes 196608 | tf_op jit(solution)/shard_map/edges/all_to_all | solution.py:272
  71.4 3.1 %lags.1 = bf16[16,64,256]{2,1,0:T(8,128)(2,1)S(1)} custom-call(s32[3,1,128]{2,1,0:T(1,128)S(4)} %get-tuple-element.8.plan_ref.refs_0_, bf16[32,72,128]{2,1,0:T(8,128)(2,1)S(1)} %all_to_all.21.refs_1_, bf16[4,96,128]{2,1,0:T(8,128)(2,1)S(1)} %all_to_all.22.refs_2_), custom_call_target="tpu_custom_call" | custom-call | tf_op jit(solution)/shard_map/lags/pallas_call | solution.py:275
  74.5 18.6 %all_to_all.23.got_ref = bf16[16,64,256]{2,1,0:T(8,128)(2,1)S(1)} all-to-all(bf16[16,64,256]{2,1,0:T(8,128)(2,1)S(1)} %lags.1), channel_id=1, replica_groups=mesh['y'=4,'zh'=4,'core'=2,'zl'=4,'x'=4] {'zl','x'}, dimensions={0} | all-to-all | bytes 1048576 | tf_op jit(solution)/shard_map/reduce/all_to_all | solution.py:288
  93.1 1.0 %finish.1 = f32[4,16,1024]{2,1,0:T(8,128)} custom-call(bf16[16,64,256]{2,1,0:T(8,128)(2,1)S(1)} %all_to_all.23.got_ref), custom_call_target="tpu_custom_call" | custom-call | tf_op jit(solution)/shard_map/finish/pallas_call | solution.py:289
  (6 shorter events, 0.1 us)

commit v8 on v6

--- a/solution.py
+++ b/solution.py
@@ -43,10 +43,9 @@
         spread = spread + jnp.sum(piece * piece, axis=1, keepdims=True)
         out_ref[part] = piece.astype(jnp.bfloat16)
     lane = lax.broadcasted_iota(jnp.int32, (rows, LANES), 1)
-    columns = jnp.where(lane == 0, mean, jnp.where(lane == 1, spread, 0.0))
-    turned = jnp.transpose(jnp.concatenate([columns] * (LANES // rows), axis=0))
-    wide = lax.broadcasted_iota(jnp.int32, (1, LANES), 1)
-    line = jnp.where(wide < rows, turned[0:1], turned[1:2])
+    channel = lax.broadcasted_iota(jnp.int32, (rows, LANES), 0)
+    placed = jnp.where(lane == channel, mean, jnp.where(lane == channel + rows, spread, 0.0))
+    line = jnp.sum(placed, axis=0, keepdims=True)
     high = line.astype(jnp.bfloat16).astype(jnp.float32)
     middle = (line - high).astype(jnp.bfloat16).astype(jnp.float32)
     low = line - high - middle
@@ -74,9 +73,9 @@
         return data, lines
 
     for index in range(CHUNKS):
-        place = index // X
+        place = index % EIGHTHS
         pair = ((place // CORE * ZH + zh) * CORE) + place % CORE
-        tile = pair * X + index % X
+        tile = pair * X + index // EIGHTHS
         first = plan_ref[0, 0, tile]
         data, lines = fetch(first)
         data_second, lines_second = fetch(first + plan_ref[1, 0, tile])
@@ -86,7 +85,7 @@
 
 
 def chunk_place(chunk):
-    return chunk % EIGHTHS * X + chunk // EIGHTHS
+    return chunk
 
 
 def scales(edge_ref, first_half, second_half, zl, length):
@@ -266,9 +265,10 @@
         name="select",
     )(pltpu.with_memory_space_constraint(plan, pltpu.SMEM), table)
     with jax.named_scope("collect"):
-        data = lax.all_to_all(chosen, ("y", "core", "x"), 0, 0, tiled=True)
+        data = lax.all_to_all(chosen, ("x", "y", "core"), 0, 0, tiled=True)
     with jax.named_scope("edges"):
-        sums = jnp.sum(data[:, 2 * CB :].reshape(EIGHTHS, X * EXTRA, LANES), axis=0)
+        sums = jnp.sum(data[:, 2 * CB :].reshape(X, EIGHTHS, EXTRA, LANES), axis=1)
+        sums = sums.reshape(X * EXTRA, LANES)
         edges = jnp.concatenate(
             [data[chunk_place(0), CB : 2 * CB], data[chunk_place(CHUNKS - 1), CB : 2 * CB], sums]
         )

time: 94.3 us -> 94.7 us (level)
  the two profiles are of different devices: /device:TPU:32 before, /device:TPU:8 now
where the time goes in v8:
time: 94.7 us; the launch traced here: 94.5 us
  blocking collectives  88.6 us (94%)
  Pallas kernels  5.81 us (6%)
    all_gather x1, blocking collectives, body(): table = lax.all_gather(table, 'zh')  29.2 us
    all_to_all x1, blocking collectives, body(): got = lax.all_to_all(partial, ('zl', 'x'), 0, 0, tiled=True)  19.5 us
    all_to_all x1, blocking collectives, body(): data = lax.all_to_all(chosen, ('x', 'y', 'core'), 0, 0, tiled=True)  18.6 us
    all_to_all x1, blocking collectives, body(): table = lax.all_to_all(parts, ('y', 'core'), 0, 0, tiled=True)  12.9 us
    all_to_all x1, blocking collectives, body(): lax.all_to_all(jnp.broadcast_to(edges[None], (ZL,) + edges.shape), 'zl',...  8.36 us
    pallas_call x1, Pallas kernels, body(): pl.pallas_call(lambda *refs: lag_kernel(length, *refs), out_shape=jax.Sha...  3.07 us

profile of v8, /device:TPU:8, one launch (start us, length us, event | category | flops | bytes accessed | tf_op | source)
XLA Modules:
  0.0 94.5 jit_solution(13045932951424337644)
XLA Ops:
  0.0 1.3 %split.1 = (bf16[8,64,128]{2,1,0:T(8,128)(2,1)S(1)}, bf16[8,128]{1,0:T(8,128)(2,1)S(1)}, s32[3,1,128]{2,1,0:T(1,128)S(4)}) custom-call(f32[64,1024]{1,0:T(8,128)} %x_hbm.1, s32[1,128]{1,0:T(1,128)} %bitcast.15, s32[1,128]{1,0:T(1,128)} %bitcast.16, s32[1,128]{1,0:T(1,128)} %bitcast.17), custom_call_target="tpu_custom_call" | custom-call | tf_op jit(solution)/shard_map/split/pallas_call | solution.py:233
  1.3 12.9 %all_to_all.20 = bf16[8,64,128]{2,1,0:T(8,128)(2,1)S(1)} all-to-all(bf16[8,64,128]{2,1,0:T(8,128)(2,1)S(1)} %get-tuple-element.9), channel_id=1, replica_groups=mesh['y'=4,'zh'=4,'core'=2,'zl'=4,'x'=4] {'y','core'}, dimensions={0} | all-to-all | bytes 262144 | tf_op jit(solution)/shard_map/spread_y/all_to_all | solution.py:255
  14.2 29.2 %all-gather = bf16[2080,128]{1,0:T(8,128)(2,1)S(1)} all-gather(bf16[520,128]{1,0:T(8,128)(2,1)S(1)} %pad_maximum_fusion), channel_id=2, replica_groups=mesh['y'=4,'zh'=4,'core'=2,'zl'=4,'x'=4] {'zh'}, dimensions={0}, use_global_device_ids=true | all-gather | bytes 665600 | tf_op jit(solution)/shard_map/spread_z/all_gather | solution.py:258
  43.3 0.5 select.1
  43.9 18.6 %all_to_all.21.refs_1_ = bf16[32,72,128]{2,1,0:T(8,128)(2,1)S(1)} all-to-all(bf16[32,72,128]{2,1,0:T(8,128)(2,1)S(1)} %select.1), channel_id=1, replica_groups=mesh['y'=4,'zh'=4,'core'=2,'zl'=4,'x'=4] {'x','y','core'}, dimensions={0} | all-to-all | bytes 1179648 | tf_op jit(solution)/shard_map/collect/all_to_all | solution.py:268
  62.5 8.4 %all_to_all.22.refs_2_ = bf16[4,96,128]{2,1,0:T(8,128)(2,1)S(1)} all-to-all(bf16[4,96,128]{2,1,0:T(8,128)(2,1)S(1)} %broadcast_in_dim.18), channel_id=1, replica_groups=mesh['y'=4,'zh'=4,'core'=2,'zl'=4,'x'=4] {'zl'}, dimensions={0} | all-to-all | bytes 196608 | tf_op jit(solution)/shard_map/edges/all_to_all | solution.py:275
  70.9 3.1 %lags.1 = bf16[16,64,256]{2,1,0:T(8,128)(2,1)S(1)} custom-call(s32[3,1,128]{2,1,0:T(1,128)S(4)} %get-tuple-element.8.plan_ref.refs_0_, bf16[32,72,128]{2,1,0:T(8,128)(2,1)S(1)} %all_to_all.21.refs_1_, bf16[4,96,128]{2,1,0:T(8,128)(2,1)S(1)} %all_to_all.22.refs_2_), custom_call_target="tpu_custom_call" | custom-call | tf_op jit(solution)/shard_map/lags/pallas_call | solution.py:278
  74.0 19.5 %all_to_all.23.got_ref = bf16[16,64,256]{2,1,0:T(8,128)(2,1)S(1)} all-to-all(bf16[16,64,256]{2,1,0:T(8,128)(2,1)S(1)} %lags.1), channel_id=1, replica_groups=mesh['y'=4,'zh'=4,'core'=2,'zl'=4,'x'=4] {'zl','x'}, dimensions={0} | all-to-all | bytes 1048576 | tf_op jit(solution)/shard_map/reduce/all_to_all | solution.py:291
  93.5 1.0 %finish.1 = f32[4,16,1024]{2,1,0:T(8,128)} custom-call(bf16[16,64,256]{2,1,0:T(8,128)(2,1)S(1)} %all_to_all.23.got_ref), custom_call_target="tpu_custom_call" | custom-call | tf_op jit(solution)/shard_map/finish/pallas_call | solution.py:292
  (5 shorter events, 0.0 us)

commit v9 on v6

--- a/solution.py
+++ b/solution.py
@@ -20,6 +20,7 @@
 FINE = 8
 MEDIUM = LANES // FINE
 EXTRA = 8
+STRIPS = 4
 ROWS = 2 * CB + EXTRA
 MIB = 1 << 20
 
@@ -30,12 +31,16 @@
 
 def split_kernel(x_hbm, rows_hbm, offsets_hbm, live_hbm, out_ref, extra_ref, plan_ref, x_ref, sems):
     rows, length = x_ref.shape
-    copies = [pltpu.make_async_copy(x_hbm, x_ref, sems.at[0])]
+    copies = []
+    for strip in range(STRIPS):
+        part = pl.ds(strip * (rows // STRIPS), rows // STRIPS)
+        copies.append(pltpu.make_async_copy(x_hbm.at[part], x_ref.at[part], sems.at[strip]))
     for place, ref in enumerate((rows_hbm, offsets_hbm, live_hbm)):
-        copies.append(pltpu.make_async_copy(ref, plan_ref.at[place], sems.at[place + 1]))
+        copies.append(pltpu.make_async_copy(ref, plan_ref.at[place], sems.at[STRIPS + place]))
     for copy in copies:
         copy.start()
-    copies[0].wait()
+    for copy in copies[:STRIPS]:
+        copy.wait()
     mean = jnp.sum(x_ref[...], axis=1, keepdims=True) / length
     spread = jnp.zeros((rows, 1), jnp.float32)
     for part in range(EIGHTHS):
@@ -43,17 +48,16 @@
         spread = spread + jnp.sum(piece * piece, axis=1, keepdims=True)
         out_ref[part] = piece.astype(jnp.bfloat16)
     lane = lax.broadcasted_iota(jnp.int32, (rows, LANES), 1)
-    columns = jnp.where(lane == 0, mean, jnp.where(lane == 1, spread, 0.0))
-    turned = jnp.transpose(jnp.concatenate([columns] * (LANES // rows), axis=0))
-    wide = lax.broadcasted_iota(jnp.int32, (1, LANES), 1)
-    line = jnp.where(wide < rows, turned[0:1], turned[1:2])
+    channel = lax.broadcasted_iota(jnp.int32, (rows, LANES), 0)
+    placed = jnp.where(lane == channel, mean, jnp.where(lane == channel + rows, spread, 0.0))
+    line = jnp.sum(placed, axis=0, keepdims=True)
     high = line.astype(jnp.bfloat16).astype(jnp.float32)
     middle = (line - high).astype(jnp.bfloat16).astype(jnp.float32)
     low = line - high - middle
     row = lax.broadcasted_iota(jnp.int32, (EXTRA, LANES), 0) % (EXTRA // 2)
     lines = jnp.where(row == 0, high, jnp.where(row == 1, middle, jnp.where(row == 2, low, 0.0)))
     extra_ref[...] = lines.astype(jnp.bfloat16)
-    for copy in copies[1:]:
+    for copy in copies[STRIPS:]:
         copy.wait()
 
 
@@ -146,21 +150,24 @@
         zero = jnp.zeros((CB, LANES), jnp.bfloat16)
         first_scale, second_scale = scales(edge_ref, first_half, second_half, zl, length)
 
-        def white(piece, scale, column):
+        first_by = first_scale[:, 0:1] * factor
+        second_by = second_scale[:, 0:1]
+
+        def white(piece, scale, column, by):
             shifted = piece.astype(jnp.float32) + scale[:, column + 2 : column + 3]
-            return (shifted * scale[:, 0:1]).astype(jnp.bfloat16)
+            return (shifted * by).astype(jnp.bfloat16)
 
         def first_chunk(chunk):
-            return white(data_ref[chunk_place(chunk), :CB], first_scale, chunk // EIGHTHS)
+            return white(data_ref[chunk_place(chunk), :CB], first_scale, chunk // EIGHTHS, first_by)
 
         def second_chunk(chunk):
             if chunk < 0:
-                piece = white(edge_ref[jnp.maximum(zl - 1, 0), CB : 2 * CB], second_scale, -1)
+                piece = white(edge_ref[jnp.maximum(zl - 1, 0), CB : 2 * CB], second_scale, -1, second_by)
                 return jnp.where(zl > 0, piece, zero)
             if chunk >= CHUNKS:
-                piece = white(edge_ref[jnp.minimum(zl + 1, ZL - 1), :CB], second_scale, X)
+                piece = white(edge_ref[jnp.minimum(zl + 1, ZL - 1), :CB], second_scale, X, second_by)
                 return jnp.where(zl < ZL - 1, piece, zero)
-            return white(data_ref[chunk_place(chunk), CB : 2 * CB], second_scale, chunk // EIGHTHS)
+            return white(data_ref[chunk_place(chunk), CB : 2 * CB], second_scale, chunk // EIGHTHS, second_by)
 
         here = zero
         for chunk in range(CHUNKS + 1):
@@ -188,7 +195,7 @@
                 (((1,), (1,)), ((), ())),
                 preferred_element_type=jnp.float32,
             )
-            rounded = (result * factor).astype(jnp.bfloat16)
+            rounded = result.astype(jnp.bfloat16)
             for part in range(TMS // 2):
                 out_ref[half * (TMS // 2) + part] = rounded[part * 2 * CB : (part + 1) * 2 * CB]
 
@@ -242,7 +249,7 @@
         out_specs=(VMEM, VMEM, SMEM),
         scratch_shapes=[
             pltpu.VMEM(samples.shape, jnp.float32),
-            pltpu.SemaphoreType.DMA((4,)),
+            pltpu.SemaphoreType.DMA((STRIPS + 3,)),
         ],
         compiler_params=pltpu.CompilerParams(vmem_limit_bytes=3 * MIB),
         name="split",

time: 94.3 us -> 94.3 us (level)
  no operation moved by 1% of the time
where the time goes in v9:
time: 94.3 us; the launch traced here: 94 us
  blocking collectives  88.1 us (93%)
  Pallas kernels  5.81 us (6%)
    all_gather x1, blocking collectives, body(): table = lax.all_gather(table, 'zh')  32.4 us
    all_to_all x1, blocking collectives, body(): got = lax.all_to_all(partial, ('zl', 'x'), 0, 0, tiled=True)  18.6 us
    all_to_all x1, blocking collectives, body(): data = lax.all_to_all(chosen, ('y', 'core', 'x'), 0, 0, tiled=True)  17.5 us
    all_to_all x1, blocking collectives, body(): table = lax.all_to_all(parts, ('y', 'core'), 0, 0, tiled=True)  10.4 us
    all_to_all x1, blocking collectives, body(): lax.all_to_all(jnp.broadcast_to(edges[None], (ZL,) + edges.shape), 'zl',...  9.16 us
    pallas_call x1, Pallas kernels, body(): pl.pallas_call(lambda *refs: lag_kernel(length, *refs), out_shape=jax.Sha...  3.07 us

profile of v9, /device:TPU:32, one launch (start us, length us, event | category | flops | bytes accessed | tf_op | source)
XLA Modules:
  0.0 94.0 jit_solution(15744702471969243419)
XLA Ops:
  0.0 1.3 %split.1 = (bf16[8,64,128]{2,1,0:T(8,128)(2,1)S(1)}, bf16[8,128]{1,0:T(8,128)(2,1)S(1)}, s32[3,1,128]{2,1,0:T(1,128)S(4)}) custom-call(f32[64,1024]{1,0:T(8,128)} %x_hbm.1, s32[1,128]{1,0:T(1,128)} %bitcast.15, s32[1,128]{1,0:T(1,128)} %bitcast.16, s32[1,128]{1,0:T(1,128)} %bitcast.17), custom_call_target="tpu_custom_call" | custom-call | tf_op jit(solution)/shard_map/split/pallas_call | solution.py:241
  1.3 10.4 %all_to_all.20 = bf16[8,64,128]{2,1,0:T(8,128)(2,1)S(1)} all-to-all(bf16[8,64,128]{2,1,0:T(8,128)(2,1)S(1)} %get-tuple-element.9), channel_id=1, replica_groups=mesh['y'=4,'zh'=4,'core'=2,'zl'=4,'x'=4] {'y','core'}, dimensions={0} | all-to-all | bytes 262144 | tf_op jit(solution)/shard_map/spread_y/all_to_all | solution.py:263
  11.7 32.4 %all-gather = bf16[2080,128]{1,0:T(8,128)(2,1)S(1)} all-gather(bf16[520,128]{1,0:T(8,128)(2,1)S(1)} %pad_maximum_fusion), channel_id=2, replica_groups=mesh['y'=4,'zh'=4,'core'=2,'zl'=4,'x'=4] {'zh'}, dimensions={0}, use_global_device_ids=true | all-gather | bytes 665600 | tf_op jit(solution)/shard_map/spread_z/all_gather | solution.py:266
  44.1 0.5 select.1
  44.6 17.5 %all_to_all.21.refs_1_ = bf16[32,72,128]{2,1,0:T(8,128)(2,1)S(1)} all-to-all(bf16[32,72,128]{2,1,0:T(8,128)(2,1)S(1)} %select.1), channel_id=1, replica_groups=mesh['y'=4,'zh'=4,'core'=2,'zl'=4,'x'=4] {'y','core','x'}, dimensions={0} | all-to-all | bytes 1179648 | tf_op jit(solution)/shard_map/collect/all_to_all | solution.py:276
  62.2 9.2 %all_to_all.22.refs_2_ = bf16[4,96,128]{2,1,0:T(8,128)(2,1)S(1)} all-to-all(bf16[4,96,128]{2,1,0:T(8,128)(2,1)S(1)} %broadcast_in_dim.18), channel_id=1, replica_groups=mesh['y'=4,'zh'=4,'core'=2,'zl'=4,'x'=4] {'zl'}, dimensions={0} | all-to-all | bytes 196608 | tf_op jit(solution)/shard_map/edges/all_to_all | solution.py:282
  71.4 3.1 %lags.1 = bf16[16,64,256]{2,1,0:T(8,128)(2,1)S(1)} custom-call(s32[3,1,128]{2,1,0:T(1,128)S(4)} %get-tuple-element.8.plan_ref.refs_0_, bf16[32,72,128]{2,1,0:T(8,128)(2,1)S(1)} %all_to_all.21.refs_1_, bf16[4,96,128]{2,1,0:T(8,128)(2,1)S(1)} %all_to_all.22.refs_2_), custom_call_target="tpu_custom_call" | custom-call | tf_op jit(solution)/shard_map/lags/pallas_call | solution.py:285
  74.5 18.6 %all_to_all.23.got_ref = bf16[16,64,256]{2,1,0:T(8,128)(2,1)S(1)} all-to-all(bf16[16,64,256]{2,1,0:T(8,128)(2,1)S(1)} %lags.1), channel_id=1, replica_groups=mesh['y'=4,'zh'=4,'core'=2,'zl'=4,'x'=4] {'zl','x'}, dimensions={0} | all-to-all | bytes 1048576 | tf_op jit(solution)/shard_map/reduce/all_to_all | solution.py:298
  93.0 1.0 %finish.1 = f32[4,16,1024]{2,1,0:T(8,128)} custom-call(bf16[16,64,256]{2,1,0:T(8,128)(2,1)S(1)} %all_to_all.23.got_ref), custom_call_target="tpu_custom_call" | custom-call | tf_op jit(solution)/shard_map/finish/pallas_call | solution.py:299
  (6 shorter events, 0.1 us)

commit v10 on v9

--- a/solution.py
+++ b/solution.py
@@ -63,13 +63,13 @@
 
 def select_kernel(plan_ref, table_ref, out_ref):
     zh = lax.axis_index("zh")
-    here = lax.axis_index("y") * CORE + lax.axis_index("core")
+    here = lax.axis_index("core") * Y + lax.axis_index("y")
     bulk = EIGHTHS * 2 * CB
     row = lax.broadcasted_iota(jnp.int32, (EXTRA, LANES), 0)
 
     def fetch(block):
         block = jnp.clip(block, 0, 2 * PAIRS - 1)
-        place = ((block >> 4) << 1) | ((block >> 1) & 1)
+        place = (((block >> 1) & 1) << 2) | (block >> 4)
         column = (block >> 2) & (ZH - 1)
         start = pl.multiple_of(((place << 1) | (block & 1)) * CB, CB)
         data = table_ref[column, pl.ds(start, CB)]
@@ -79,7 +79,7 @@
 
     for index in range(CHUNKS):
         place = index // X
-        pair = ((place // CORE * ZH + zh) * CORE) + place % CORE
+        pair = ((place % Y * ZH + zh) * CORE) + place // Y
         tile = pair * X + index % X
         first = plan_ref[0, 0, tile]
         data, lines = fetch(first)
@@ -260,7 +260,7 @@
         )
     )
     with jax.named_scope("spread_y"):
-        table = lax.all_to_all(parts, ("y", "core"), 0, 0, tiled=True)
+        table = lax.all_to_all(parts, ("core", "y"), 0, 0, tiled=True)
     with jax.named_scope("spread_z"):
         table = jnp.concatenate([table.reshape(EIGHTHS * 2 * CB, LANES), lines])
         table = lax.all_gather(table, "zh")
@@ -273,7 +273,7 @@
         name="select",
     )(pltpu.with_memory_space_constraint(plan, pltpu.SMEM), table)
     with jax.named_scope("collect"):
-        data = lax.all_to_all(chosen, ("y", "core", "x"), 0, 0, tiled=True)
+        data = lax.all_to_all(chosen, ("core", "y", "x"), 0, 0, tiled=True)
     with jax.named_scope("edges"):
         sums = jnp.sum(data[:, 2 * CB :].reshape(EIGHTHS, X * EXTRA, LANES), axis=0)
         edges = jnp.concatenate(

time: 94.3 us -> 93.5 us (level)
  no operation moved by 1% of the time
where the time goes in v10:
time: 93.5 us; the launch traced here: 93.2 us
  blocking collectives  87.3 us (93%)
  Pallas kernels  5.81 us (6%)
    all_gather x1, blocking collectives, body(): table = lax.all_gather(table, 'zh')  32.4 us
    all_to_all x1, blocking collectives, body(): got = lax.all_to_all(partial, ('zl', 'x'), 0, 0, tiled=True)  18.4 us
    all_to_all x1, blocking collectives, body(): data = lax.all_to_all(chosen, ('core', 'y', 'x'), 0, 0, tiled=True)  18.4 us
    all_to_all x1, blocking collectives, body(): table = lax.all_to_all(parts, ('core', 'y'), 0, 0, tiled=True)  9.83 us
    all_to_all x1, blocking collectives, body(): lax.all_to_all(jnp.broadcast_to(edges[None], (ZL,) + edges.shape), 'zl',...  8.26 us
    pallas_call x1, Pallas kernels, body(): pl.pallas_call(lambda *refs: lag_kernel(length, *refs), out_shape=jax.Sha...  3.07 us

profile of v10, /device:TPU:32, one launch (start us, length us, event | category | flops | bytes accessed | tf_op | source)
XLA Modules:
  0.0 93.2 jit_solution(7846389244501659086)
XLA Ops:
  0.0 1.3 %split.1 = (bf16[8,64,128]{2,1,0:T(8,128)(2,1)S(1)}, bf16[8,128]{1,0:T(8,128)(2,1)S(1)}, s32[3,1,128]{2,1,0:T(1,128)S(4)}) custom-call(f32[64,1024]{1,0:T(8,128)} %x_hbm.1, s32[1,128]{1,0:T(1,128)} %bitcast.15, s32[1,128]{1,0:T(1,128)} %bitcast.16, s32[1,128]{1,0:T(1,128)} %bitcast.17), custom_call_target="tpu_custom_call" | custom-call | tf_op jit(solution)/shard_map/split/pallas_call | solution.py:241
  1.3 9.8 %all_to_all.20 = bf16[8,64,128]{2,1,0:T(8,128)(2,1)S(1)} all-to-all(bf16[8,64,128]{2,1,0:T(8,128)(2,1)S(1)} %get-tuple-element.9), channel_id=1, replica_groups=mesh['y'=4,'zh'=4,'core'=2,'zl'=4,'x'=4] {'core','y'}, dimensions={0} | all-to-all | bytes 262144 | tf_op jit(solution)/shard_map/spread_y/all_to_all | solution.py:263
  11.1 32.4 %all-gather = bf16[2080,128]{1,0:T(8,128)(2,1)S(1)} all-gather(bf16[520,128]{1,0:T(8,128)(2,1)S(1)} %pad_maximum_fusion), channel_id=2, replica_groups=mesh['y'=4,'zh'=4,'core'=2,'zl'=4,'x'=4] {'zh'}, dimensions={0}, use_global_device_ids=true | all-gather | bytes 665600 | tf_op jit(solution)/shard_map/spread_z/all_gather | solution.py:266
  43.5 0.5 select.1
  44.0 18.4 %all_to_all.21.refs_1_ = bf16[32,72,128]{2,1,0:T(8,128)(2,1)S(1)} all-to-all(bf16[32,72,128]{2,1,0:T(8,128)(2,1)S(1)} %select.1), channel_id=1, replica_groups=mesh['y'=4,'zh'=4,'core'=2,'zl'=4,'x'=4] {'core','y','x'}, dimensions={0} | all-to-all | bytes 1179648 | tf_op jit(solution)/shard_map/collect/all_to_all | solution.py:276
  62.4 8.3 %all_to_all.22.refs_2_ = bf16[4,96,128]{2,1,0:T(8,128)(2,1)S(1)} all-to-all(bf16[4,96,128]{2,1,0:T(8,128)(2,1)S(1)} %broadcast_in_dim.18), channel_id=1, replica_groups=mesh['y'=4,'zh'=4,'core'=2,'zl'=4,'x'=4] {'zl'}, dimensions={0} | all-to-all | bytes 196608 | tf_op jit(solution)/shard_map/edges/all_to_all | solution.py:282
  70.7 3.1 %lags.1 = bf16[16,64,256]{2,1,0:T(8,128)(2,1)S(1)} custom-call(s32[3,1,128]{2,1,0:T(1,128)S(4)} %get-tuple-element.8.plan_ref.refs_0_, bf16[32,72,128]{2,1,0:T(8,128)(2,1)S(1)} %all_to_all.21.refs_1_, bf16[4,96,128]{2,1,0:T(8,128)(2,1)S(1)} %all_to_all.22.refs_2_), custom_call_target="tpu_custom_call" | custom-call | tf_op jit(solution)/shard_map/lags/pallas_call | solution.py:285
  73.8 18.4 %all_to_all.23.got_ref = bf16[16,64,256]{2,1,0:T(8,128)(2,1)S(1)} all-to-all(bf16[16,64,256]{2,1,0:T(8,128)(2,1)S(1)} %lags.1), channel_id=1, replica_groups=mesh['y'=4,'zh'=4,'core'=2,'zl'=4,'x'=4] {'zl','x'}, dimensions={0} | all-to-all | bytes 1048576 | tf_op jit(solution)/shard_map/reduce/all_to_all | solution.py:298
  92.2 1.0 %finish.1 = f32[4,16,1024]{2,1,0:T(8,128)} custom-call(bf16[16,64,256]{2,1,0:T(8,128)(2,1)S(1)} %all_to_all.23.got_ref), custom_call_target="tpu_custom_call" | custom-call | tf_op jit(solution)/shard_map/finish/pallas_call | solution.py:299
  (6 shorter events, 0.1 us)

commit v11 on v10

--- a/solution.py
+++ b/solution.py
@@ -78,9 +78,9 @@
         return data, lines
 
     for index in range(CHUNKS):
-        place = index // X
+        place = index % EIGHTHS
         pair = ((place % Y * ZH + zh) * CORE) + place // Y
-        tile = pair * X + index % X
+        tile = pair * X + index // EIGHTHS
         first = plan_ref[0, 0, tile]
         data, lines = fetch(first)
         data_second, lines_second = fetch(first + plan_ref[1, 0, tile])
@@ -90,7 +90,7 @@
 
 
 def chunk_place(chunk):
-    return chunk % EIGHTHS * X + chunk // EIGHTHS
+    return chunk
 
 
 def scales(edge_ref, first_half, second_half, zl, length):
@@ -273,9 +273,10 @@
         name="select",
     )(pltpu.with_memory_space_constraint(plan, pltpu.SMEM), table)
     with jax.named_scope("collect"):
-        data = lax.all_to_all(chosen, ("core", "y", "x"), 0, 0, tiled=True)
+        data = lax.all_to_all(chosen, ("x", "core", "y"), 0, 0, tiled=True)
     with jax.named_scope("edges"):
-        sums = jnp.sum(data[:, 2 * CB :].reshape(EIGHTHS, X * EXTRA, LANES), axis=0)
+        sums = jnp.sum(data[:, 2 * CB :].reshape(X, EIGHTHS, EXTRA, LANES), axis=1)
+        sums = sums.reshape(X * EXTRA, LANES)
         edges = jnp.concatenate(
             [data[chunk_place(0), CB : 2 * CB], data[chunk_place(CHUNKS - 1), CB : 2 * CB], sums]
         )

time: 93.5 us -> 93.3 us (level)
  no operation moved by 1% of the time
where the time goes in v11:
time: 93.3 us; the launch traced here: 93 us
  blocking collectives  87.1 us (93%)
  Pallas kernels  5.82 us (6%)
    all_gather x1, blocking collectives, body(): table = lax.all_gather(table, 'zh')  32.4 us
    all_to_all x1, blocking collectives, body(): got = lax.all_to_all(partial, ('zl', 'x'), 0, 0, tiled=True)  18.5 us
    all_to_all x1, blocking collectives, body(): data = lax.all_to_all(chosen, ('x', 'core', 'y'), 0, 0, tiled=True)  18.2 us
    all_to_all x1, blocking collectives, body(): table = lax.all_to_all(parts, ('core', 'y'), 0, 0, tiled=True)  9.83 us
    all_to_all x1, blocking collectives, body(): lax.all_to_all(jnp.broadcast_to(edges[None], (ZL,) + edges.shape), 'zl',...  8.26 us
    pallas_call x1, Pallas kernels, body(): pl.pallas_call(lambda *refs: lag_kernel(length, *refs), out_shape=jax.Sha...  3.07 us

profile of v11, /device:TPU:32, one launch (start us, length us, event | category | flops | bytes accessed | tf_op | source)
XLA Modules:
  0.0 93.0 jit_solution(5350151145163323618)
XLA Ops:
  0.0 1.3 %split.1 = (bf16[8,64,128]{2,1,0:T(8,128)(2,1)S(1)}, bf16[8,128]{1,0:T(8,128)(2,1)S(1)}, s32[3,1,128]{2,1,0:T(1,128)S(4)}) custom-call(f32[64,1024]{1,0:T(8,128)} %x_hbm.1, s32[1,128]{1,0:T(1,128)} %bitcast.15, s32[1,128]{1,0:T(1,128)} %bitcast.16, s32[1,128]{1,0:T(1,128)} %bitcast.17), custom_call_target="tpu_custom_call" | custom-call | tf_op jit(solution)/shard_map/split/pallas_call | solution.py:241
  1.3 9.8 %all_to_all.20 = bf16[8,64,128]{2,1,0:T(8,128)(2,1)S(1)} all-to-all(bf16[8,64,128]{2,1,0:T(8,128)(2,1)S(1)} %get-tuple-element.9), channel_id=1, replica_groups=mesh['y'=4,'zh'=4,'core'=2,'zl'=4,'x'=4] {'core','y'}, dimensions={0} | all-to-all | bytes 262144 | tf_op jit(solution)/shard_map/spread_y/all_to_all | solution.py:263
  11.1 32.4 %all-gather = bf16[2080,128]{1,0:T(8,128)(2,1)S(1)} all-gather(bf16[520,128]{1,0:T(8,128)(2,1)S(1)} %pad_maximum_fusion), channel_id=2, replica_groups=mesh['y'=4,'zh'=4,'core'=2,'zl'=4,'x'=4] {'zh'}, dimensions={0}, use_global_device_ids=true | all-gather | bytes 665600 | tf_op jit(solution)/shard_map/spread_z/all_gather | solution.py:266
  43.5 0.5 select.1
  44.0 18.2 %all_to_all.21.refs_1_ = bf16[32,72,128]{2,1,0:T(8,128)(2,1)S(1)} all-to-all(bf16[32,72,128]{2,1,0:T(8,128)(2,1)S(1)} %select.1), channel_id=1, replica_groups=mesh['y'=4,'zh'=4,'core'=2,'zl'=4,'x'=4] {'x','core','y'}, dimensions={0} | all-to-all | bytes 1179648 | tf_op jit(solution)/shard_map/collect/all_to_all | solution.py:276
  62.2 8.3 %all_to_all.22.refs_2_ = bf16[4,96,128]{2,1,0:T(8,128)(2,1)S(1)} all-to-all(bf16[4,96,128]{2,1,0:T(8,128)(2,1)S(1)} %broadcast_in_dim.18), channel_id=1, replica_groups=mesh['y'=4,'zh'=4,'core'=2,'zl'=4,'x'=4] {'zl'}, dimensions={0} | all-to-all | bytes 196608 | tf_op jit(solution)/shard_map/edges/all_to_all | solution.py:283
  70.5 3.1 %lags.1 = bf16[16,64,256]{2,1,0:T(8,128)(2,1)S(1)} custom-call(s32[3,1,128]{2,1,0:T(1,128)S(4)} %get-tuple-element.8.plan_ref.refs_0_, bf16[32,72,128]{2,1,0:T(8,128)(2,1)S(1)} %all_to_all.21.refs_1_, bf16[4,96,128]{2,1,0:T(8,128)(2,1)S(1)} %all_to_all.22.refs_2_), custom_call_target="tpu_custom_call" | custom-call | tf_op jit(solution)/shard_map/lags/pallas_call | solution.py:286
  73.6 18.5 %all_to_all.23.got_ref = bf16[16,64,256]{2,1,0:T(8,128)(2,1)S(1)} all-to-all(bf16[16,64,256]{2,1,0:T(8,128)(2,1)S(1)} %lags.1), channel_id=1, replica_groups=mesh['y'=4,'zh'=4,'core'=2,'zl'=4,'x'=4] {'zl','x'}, dimensions={0} | all-to-all | bytes 1048576 | tf_op jit(solution)/shard_map/reduce/all_to_all | solution.py:299
  92.0 1.0 %finish.1 = f32[4,16,1024]{2,1,0:T(8,128)} custom-call(bf16[16,64,256]{2,1,0:T(8,128)(2,1)S(1)} %all_to_all.23.got_ref), custom_call_target="tpu_custom_call" | custom-call | tf_op jit(solution)/shard_map/finish/pallas_call | solution.py:300
  (5 shorter events, 0.0 us)
